TPU v7x, 32 devices: a whole 2x2x4 slice. The times are simulated.
32 devices in a mesh: gx: 16 (over z, x, core), gy: 2 (over y).
Axes of the slice: x: 2, y: 2, z: 4, core: 2. Of those that a mesh axis runs over, the one named last changes fastest.
Arguments:
- tokens: bfloat16 [2304, 4608], P('gx', 'gy'), may hold values from -6 to 6
- pre_gain: bfloat16 [4608], P('gy'), may hold values from -0.5 to 0.5
- w_q: bfloat16 [4608, 4096], P('gx', 'gy'), may hold values from -0.09375 to 0.09375
- w_k: bfloat16 [4608, 2048], P('gx', 'gy'), may hold values from -0.09375 to 0.09375
- w_v: bfloat16 [4608, 2048], P('gx', 'gy'), may hold values from -0.09375 to 0.09375
- w_o: bfloat16 [4096, 4608], P('gy', 'gx')
- post_gain: bfloat16 [4608], P('gy'), may hold values from -0.5 to 0.5
- k_cache: bfloat16 [16384, 2048], P('gx', 'gy'), may hold values from -6 to 6
- v_cache: bfloat16 [16384, 2048], P('gx', 'gy')
- cached_len: int32 [12], replicated, may hold values from 1 to 5120, as said below
- new_len: int32 [12], replicated, may hold values from 48 to 192, as said below
- slot_offset: int32 [12], replicated, may hold values from 0 to 16191, as said below
Outputs:
- layer_out: bfloat16 [2304, 4608], P('gx', 'gy')
- k_pool: bfloat16 [16384, 2048], P('gx', 'gy')
- v_pool: bfloat16 [16384, 2048], P('gx', 'gy')
Inputs may be any that keep to these rules, and one draw needn't show every extreme that they name: `cached_len`: two requests are long: one has exactly 5120 cached tokens, the other between 4929 and 5120; the others have at most 256, and one of them has exactly 1. `new_len`: some request has all 192 slots real. Request r owns pool slots slot_offset[r] to slot_offset[r] + cached_len[r] + 191; these regions are disjoint and lie inside the pool; one starts at slot 0 and one ends at the pool's last slot.
All inputs are finite; a program needn't handle non-finite values.
Results may differ from a plain program's by a relative error of at most 0.02.
Values may be sent and summed in bfloat16 or wider, within the bound.
A program may use at most 128 MiB of HBM per device.

v0:
```python
import jax
import jax.numpy as jnp
from jax import lax
from jax.sharding import PartitionSpec as P

D = 4608
HD = 128
REQS = 12
NEWTOK = 192


epsilon = 1e-06
soft_cap = 50.0
query_scale = 144.0 ** (-0.5)


def rotate(values, position, head_size):
    rows = values.shape[0]
    parts = values.reshape(rows, -1, head_size)
    half = head_size // 2
    inverse = jnp.power(10000.0, -2.0 * jnp.arange(half, dtype=jnp.float32) / head_size)
    angle = position.astype(jnp.float32)[:, None] * inverse[None, :]
    cosine = jnp.cos(angle)[:, None, :]
    sine = jnp.sin(angle)[:, None, :]
    first = parts[:, :, :half]
    second = parts[:, :, half:]
    turned = jnp.concatenate(
        [first * cosine - second * sine, second * cosine + first * sine], axis=2
    )
    return turned.reshape(rows, -1)


def on_device(
    tokens,
    pre_gain,
    w_q,
    w_k,
    w_v,
    w_o,
    post_gain,
    k_cache,
    v_cache,
    cached_len,
    new_len,
    slot_offset,
):
    tok_rows = tokens.shape[0]
    whole_in, whole_gain = (
        lax.all_gather(tokens, "gy", axis=1, tiled=True),
        lax.all_gather(pre_gain, "gy", axis=0, tiled=True),
    )
    float_in = whole_in.astype(jnp.float32)
    scale_rows = lax.rsqrt(jnp.mean(float_in * float_in, axis=1, keepdims=True) + epsilon)
    normed = (float_in * scale_rows * (1.0 + whole_gain.astype(jnp.float32))).astype(jnp.bfloat16)
    q_lin = jnp.dot(
        normed, lax.all_gather(w_q, "gx", axis=0, tiled=True), preferred_element_type=jnp.float32
    )
    k_lin = jnp.dot(
        normed, lax.all_gather(w_k, "gx", axis=0, tiled=True), preferred_element_type=jnp.float32
    )
    v_lin = jnp.dot(
        normed, lax.all_gather(w_v, "gx", axis=0, tiled=True), preferred_element_type=jnp.float32
    )
    row_ids = lax.axis_index("gx") * tok_rows + jnp.arange(tok_rows, dtype=jnp.int32)
    request = row_ids // NEWTOK
    within = row_ids % NEWTOK
    owner_mask = request[:, None] == jnp.arange(REQS, dtype=jnp.int32)[None, :]
    row_cached = jnp.sum(jnp.where(owner_mask, cached_len[None, :], 0), axis=1)
    row_fresh = jnp.sum(jnp.where(owner_mask, new_len[None, :], 0), axis=1)
    position = row_cached + within
    q_new = (rotate(q_lin, position, HD) * query_scale).astype(jnp.bfloat16)
    k_new = rotate(k_lin, position, HD).astype(jnp.bfloat16)
    v_new = v_lin.astype(jnp.bfloat16)
    q_all, k_all, v_all = (
        lax.all_gather(q_new, "gx", axis=0, tiled=True),
        lax.all_gather(k_new, "gx", axis=0, tiled=True),
        lax.all_gather(v_new, "gx", axis=0, tiled=True),
    )
    slab_size = k_cache.shape[0]
    first_slot = lax.axis_index("gx") * slab_size
    slot_ids = first_slot + jnp.arange(slab_size, dtype=jnp.int32)
    offset_in = slot_ids[:, None] - slot_offset[None, :] - cached_len[None, :]
    landing = (offset_in >= 0) & (offset_in < new_len[None, :])
    source = jnp.sum(
        jnp.where(landing, jnp.arange(REQS, dtype=jnp.int32)[None, :] * NEWTOK + offset_in, 0),
        axis=1,
    )
    written = jnp.any(landing, axis=1)
    k_pool = jnp.where(written[:, None], jnp.take(k_all, source, axis=0), k_cache)
    v_pool = jnp.where(written[:, None], jnp.take(v_all, source, axis=0), v_cache)
    heads_dev = q_all.shape[1] // HD
    kv_dev = k_all.shape[1] // HD
    group_size = heads_dev // kv_dev
    kblock = min(512, slab_size)
    nblocks = slab_size // kblock
    key_blocks = k_pool.reshape(nblocks, kblock, kv_dev, HD)
    value_blocks = v_pool.reshape(nblocks, kblock, kv_dev, HD)
    total_rows = q_all.shape[0]

    def request_step(request_id, carry):
        numer_all, denom_all = carry
        first_row = request_id * NEWTOK
        rows = lax.dynamic_slice_in_dim(q_all, first_row, NEWTOK, 0).reshape(
            NEWTOK, kv_dev, group_size, HD
        )
        offset = slot_offset[request_id]
        cached = cached_len[request_id]
        fresh_count = new_len[request_id]
        last_seen = cached + jnp.minimum(jnp.arange(NEWTOK, dtype=jnp.int32), fresh_count - 1)
        region_end = offset + cached + fresh_count

        def block_terms(block, running):
            numerator, denominator = running
            key_rows = lax.dynamic_index_in_dim(key_blocks, block, 0, keepdims=False)
            value_rows = lax.dynamic_index_in_dim(value_blocks, block, 0, keepdims=False)
            key_pos = first_slot + block * kblock + jnp.arange(kblock, dtype=jnp.int32) - offset
            visible = (key_pos[None, :] >= 0) & (key_pos[None, :] <= last_seen[:, None])
            logits = jnp.einsum(
                "cgjd,sgd->cgjs", rows, key_rows, preferred_element_type=jnp.float32
            )
            weight = jnp.where(
                visible[:, None, None, :], jnp.exp(soft_cap * jnp.tanh(logits / soft_cap)), 0.0
            )
            denominator = denominator + jnp.sum(weight, axis=3)
            numerator = numerator + jnp.einsum(
                "cgjs,sgd->cgjd",
                weight.astype(jnp.bfloat16),
                value_rows,
                preferred_element_type=jnp.float32,
            )
            return (numerator, denominator)

        def compute(running):
            return lax.fori_loop(0, nblocks, block_terms, running)

        def skipped(running):
            return running

        initial = (
            jnp.zeros((NEWTOK, kv_dev, group_size, HD), jnp.float32),
            jnp.zeros((NEWTOK, kv_dev, group_size), jnp.float32),
        )
        present = (offset < first_slot + slab_size) & (region_end > first_slot)
        numerator, denominator = lax.cond(present, compute, skipped, initial)
        numer_all = lax.dynamic_update_slice_in_dim(
            numer_all, numerator.reshape(NEWTOK, heads_dev * HD), first_row, 0
        )
        denom_all = lax.dynamic_update_slice_in_dim(
            denom_all, denominator.reshape(NEWTOK, heads_dev), first_row, 0
        )
        return (numer_all, denom_all)

    start_sums = (
        jnp.zeros((total_rows, heads_dev * HD), jnp.float32),
        jnp.zeros((total_rows, heads_dev), jnp.float32),
    )
    numer_all, denom_all = lax.fori_loop(0, REQS, request_step, start_sums)
    head_num, head_den = (
        lax.psum_scatter(
            numer_all.astype(jnp.bfloat16), "gx", scatter_dimension=0, tiled=True
        ).astype(jnp.float32),
        lax.psum_scatter(
            denom_all.astype(jnp.bfloat16), "gx", scatter_dimension=0, tiled=True
        ).astype(jnp.float32),
    )
    attended = head_num.reshape(tok_rows, heads_dev, HD) / head_den[:, :, None]
    attended = jnp.where((within < row_fresh)[:, None, None], attended, 0.0)
    attended = attended.reshape(tok_rows, heads_dev * HD).astype(jnp.bfloat16)
    partial_out = jnp.dot(
        attended, lax.all_gather(w_o, "gx", axis=1, tiled=True), preferred_element_type=jnp.float32
    )
    branch = lax.psum_scatter(
        partial_out.astype(jnp.bfloat16), "gy", scatter_dimension=1, tiled=True
    ).astype(jnp.float32)
    mean_square = lax.psum(jnp.sum(branch * branch, axis=1), "gy") / D
    layer_out = (
        tokens.astype(jnp.float32)
        + branch * lax.rsqrt(mean_square + epsilon)[:, None] * (1.0 + post_gain.astype(jnp.float32))
    ).astype(jnp.bfloat16)
    return (layer_out, k_pool, v_pool)


def solution(mesh):
    placed = (
        P("gx", "gy"),
        P("gy"),
        P("gx", "gy"),
        P("gx", "gy"),
        P("gx", "gy"),
        P("gy", "gx"),
        P("gy"),
        P("gx", "gy"),
        P("gx", "gy"),
        P(),
        P(),
        P(),
    )
    return jax.shard_map(
        on_device,
        mesh=mesh,
        in_specs=placed,
        out_specs=(P("gx", "gy"), P("gx", "gy"), P("gx", "gy")),
        check_vma=False,
    )
```

profile of v0, /device:TPU:0, one launch (start us, length us, event | category | flops | bytes accessed | tf_op | source)
XLA Modules:
  0.0 1006.4 jit_solution(17784520724525812372)
XLA Ops:
  7.2 0.7 all-gather.10.cloned.1.call-update
  8.0 0.7 all-gather.20.cloned.1.call-update
  8.7 0.7 all-gather.16.cloned.1.call-update
  10.1 5.3 all-gather
  16.5 20.2 %all-gather.10.cloned.1.call-done = bf16[144,4608]{1,0:T(8,128)(2,1)} async-done(((bf16[144,2304]{1,0:T(8,128)(2,1)}), bf16[144,4608]{1,0:T(8,128)(2,1)}) %all-gather.10.cloned.1.call-update) | async-done | bytes 1327120 | tf_op jit(solution)/shard_map/all_gather | solution.py:49
  36.7 1.7 fusion.17
  38.4 82.1 %all-gather.20.cloned.1.call-done = bf16[4608,1024]{1,0:T(8,128)(2,1)} async-done(((bf16[288,1024]{1,0:T(8,128)(2,1)}), bf16[4608,1024]{1,0:T(8,128)(2,1)}) %all-gather.20.cloned.1.call-update) | async-done | bytes 9437200 | tf_op jit(solution)/shard_map/all_gather | solution.py:59
  120.5 5.7 convolution_bitcast_fusion.1
  126.8 0.8 copy.50
  127.6 74.8 %all-gather.16.cloned.1.call-done = bf16[4608,1024]{1,0:T(8,128)(2,1)} async-done(((bf16[288,1024]{1,0:T(8,128)(2,1)}), bf16[4608,1024]{1,0:T(8,128)(2,1)}) %all-gather.16.cloned.1.call-update) | async-done | bytes 9437200 | tf_op jit(solution)/shard_map/all_gather | solution.py:62
  202.4 6.1 convolution_convert_fusion.1
  208.5 92.4 %all-gather.12.cloned.1.call-done = bf16[4608,2048]{1,0:T(8,128)(2,1)} async-done(((bf16[288,2048]{1,0:T(8,128)(2,1)}), bf16[4608,2048]{1,0:T(8,128)(2,1)}) %all-gather.12.cloned.1.call-update) | async-done | bytes 18874384 | tf_op jit(solution)/shard_map/all_gather | solution.py:56
  301.0 8.0 convolution_bitcast_fusion
  310.0 1.0 copy.49
  311.3 45.6 %all-gather.22.cloned.1.call-done = bf16[2304,1024]{1,0:T(8,128)(2,1)} async-done(((bf16[144,1024]{1,0:T(8,128)(2,1)}), bf16[2304,1024]{1,0:T(8,128)(2,1)}) %all-gather.22.cloned.1.call-update) | async-done | bytes 4718608 | tf_op jit(solution)/shard_map/all_gather | solution.py:76
  356.9 8.1 gather_fusion.1
  365.1 46.4 %all-gather.18.cloned.1.call-done = bf16[2304,1024]{1,0:T(8,128)(2,1)} async-done(((bf16[144,1024]{1,0:T(8,128)(2,1)}), bf16[2304,1024]{1,0:T(8,128)(2,1)}) %all-gather.18.cloned.1.call-update) | async-done | bytes 4718608 | tf_op jit(solution)/shard_map/all_gather | solution.py:77
  411.5 8.9 gather_fusion
  420.4 3.7 select_select_fusion
  424.8 0.7 copy-done.1
  425.5 1.7 copy.31
  427.8 1.8 copy.32
  429.7 64.7 %all-gather.14.cloned.1.call-done = bf16[2304,2048]{1,0:T(8,128)(2,1)} async-done(((bf16[144,2048]{1,0:T(8,128)(2,1)}), bf16[2304,2048]{1,0:T(8,128)(2,1)}) %all-gather.14.cloned.1.call-update) | async-done | bytes 9437200 | tf_op jit(solution)/shard_map/all_gather | solution.py:75
  494.4 4.9 broadcast_in_dim.122
  499.3 128.6 %while.39 = (s32[]{:T(128)}, bf16[2304,2048]{1,0:T(8,128)(2,1)}, bf16[2304,16]{0,1:T(8,128)(2,1)S(1)}, s32[12]{0:T(128)S(1)}, s32[]{:T(128)}, /*index=5*/s32[12]...) while((s32[]{:T(128)}, bf16[2304,2048]{1,0:T(8,128)(2,1)}, ...), condition=%wide.region_11.13_spmd, body=%wide.region_5.12_spmd.sunk | while | flops 818878336 | bytes 29221012 | solution.py:157
  503.8 0.9 constant_dynamic-update-slice_fusion.2
  509.5 0.9 constant_dynamic-update-slice_fusion.2
  515.3 0.9 constant_dynamic-update-slice_fusion.2
  521.0 0.9 constant_dynamic-update-slice_fusion.2
  526.8 1.0 constant_dynamic-update-slice_fusion.2
  532.5 0.9 constant_dynamic-update-slice_fusion.2
  538.2 29.8 %conditional.2 = (bf16[192,2048]{1,0:T(8,128)(2,1)S(1)}, bf16[192,16]{0,1:T(8,128)(2,1)S(1)}) conditional(s32[]{:T(128)} %convert_element_type.140, () %tuple.101, (s32[]{:T(128)}, s32[]{:T(128)}, s32[192]{0:T(256)S(1)}, bf16[2304,2048]{1,0:T(8,128)(2,1)}, s32[]{:T(128)}, /*index=5*/bf16[2,512,8,128]{3,1,2,0:T(8,128)(2,1)}, s32[]{:T(128)}, ...), branch_computations={%region_6.7_spmd, %region_7.11_spmd} | conditional | flops 818878336 | bytes 27634232 | solution.py:144
  538.2 1.2 constant_dynamic-slice_fusion
  541.5 24.6 %while.38 = (s32[]{:T(128)}, f32[192,8,2,128]{3,0,2,1:T(8,128)S(1)}, f32[192,8,2]{0,2,1:T(2,128)S(1)}, bf16[2,512,8,128]{3,1,2,0:T(8,128)(2,1)}, s32[]{:T(128)},...) while((s32[]{:T(128)}, ...), condition=%wide.region_10.10_spmd.clone, body=%wide.region_8.9_spmd.clone.sunk | while | flops 818877952 | bytes 18963368 | solution.py:134
  543.0 5.8 fusion.54
  548.8 5.0 bitcast_add_fusion.2
  555.3 5.8 fusion.54
  561.1 5.0 bitcast_add_fusion.2
  566.1 1.2 copy.30
  568.0 0.9 constant_dynamic-update-slice_fusion.2
  573.7 1.0 constant_dynamic-update-slice_fusion.2
  579.5 1.0 constant_dynamic-update-slice_fusion.2
  585.3 0.9 constant_dynamic-update-slice_fusion.2
  591.0 29.8 %conditional.2 = (bf16[192,2048]{1,0:T(8,128)(2,1)S(1)}, bf16[192,16]{0,1:T(8,128)(2,1)S(1)}) conditional(s32[]{:T(128)} %convert_element_type.140, () %tuple.101, (s32[]{:T(128)}, s32[]{:T(128)}, s32[192]{0:T(256)S(1)}, bf16[2304,2048]{1,0:T(8,128)(2,1)}, s32[]{:T(128)}, /*index=5*/bf16[2,512,8,128]{3,1,2,0:T(8,128)(2,1)}, s32[]{:T(128)}, ...), branch_computations={%region_6.7_spmd, %region_7.11_spmd} | conditional | flops 818878336 | bytes 27634232 | solution.py:144
  591.0 1.2 constant_dynamic-slice_fusion
  594.3 24.6 %while.38 = (s32[]{:T(128)}, f32[192,8,2,128]{3,0,2,1:T(8,128)S(1)}, f32[192,8,2]{0,2,1:T(2,128)S(1)}, bf16[2,512,8,128]{3,1,2,0:T(8,128)(2,1)}, s32[]{:T(128)},...) while((s32[]{:T(128)}, ...), condition=%wide.region_10.10_spmd.clone, body=%wide.region_8.9_spmd.clone.sunk | while | flops 818877952 | bytes 18963368 | solution.py:134
  595.8 5.8 fusion.54
  601.6 5.0 bitcast_add_fusion.2
  608.1 5.8 fusion.54
  613.9 5.0 bitcast_add_fusion.2
  618.9 1.2 copy.30
  620.8 1.0 constant_dynamic-update-slice_fusion.2
  626.5 0.9 constant_dynamic-update-slice_fusion.2
  627.9 1.1 copy.36
  629.0 0.7 all-gather.24.cloned.1.call-update
  630.5 110.2 %reduce-scatter.10.cloned.1.call-done = bf16[144,16]{1,0:T(8,128)(2,1)} async-done(((bf16[2304,16]{1,0:T(8,128)(2,1)}), bf16[144,16]{1,0:T(8,128)(2,1)}) %reduce-scatter.10.cloned.1.call-update) | async-done | bytes 4624
  740.6 0.8 copy.37
  741.5 98.7 %all-gather.24.cloned.1.call-done = bf16[2048,4608]{0,1:T(8,128)(2,1)} async-done(((bf16[2048,288]{0,1:T(8,128)(2,1)}), bf16[2048,4608]{0,1:T(8,128)(2,1)}) %all-gather.24.cloned.1.call-update) | async-done | bytes 18874384 | tf_op jit(solution)/shard_map/all_gather | solution.py:170
  840.3 115.9 %reduce-scatter.6.cloned.1.call-done = bf16[144,2048]{1,0:T(8,128)(2,1)} async-done(((bf16[2304,2048]{1,0:T(8,128)(2,1)}), bf16[144,2048]{1,0:T(8,128)(2,1)}) %reduce-scatter.6.cloned.1.call-update) | async-done | bytes 589840 | tf_op jit(solution)/shard_map/reduce_scatter | solution.py:159
  956.5 11.5 %convolution_convert_fusion = bf16[144,4608]{1,0:T(8,128)(2,1)} fusion(bf16[2048,4608]{0,1:T(8,128)(2,1)} %all-gather.24.cloned.1.call-done, f32[18,8,16,128]{3,2,1,0:T(8,128)S(1)} %bitcast.91, bf16[144,2048]{1,0:T(8,128)(2,1)} %reduce-scatter.6.cloned.1.call-done, pred[144]{0:T(512)(128)(4,1)S(1)} %fusion.37), kind=kOutput, calls=%fused_computation.25 | convolution fusion | flops 2719752192 | bytes 21971088 | tf_op jit(solution)/shard_map/dot_general | solution.py:169
  968.1 23.2 %reduce-scatter.8.cloned.1.call-done = bf16[144,2304]{1,0:T(8,128)(2,1)} async-done(((bf16[144,4608]{1,0:T(8,128)(2,1)}), bf16[144,2304]{1,0:T(8,128)(2,1)}) %reduce-scatter.8.cloned.1.call-update) | async-done | bytes 663568 | tf_op jit(solution)/shard_map/reduce_scatter | solution.py:172
  991.3 1.3 fusion.20
  992.6 4.9 psum.7
  997.6 2.3 fusion.23
  (186 shorter events, 42.7 us)
Async XLA Ops:
  7.2 2.9 copy-start.4
  7.2 8.3 copy-start.7
  7.2 8.3 copy-start.6
  7.2 29.6 %all-gather.10.cloned.1.call-start = ((), (), s32[]{:S(2)}) async-start(), calls=%async_computation.3 | async-start | bytes 1990656 | tf_op jit(solution)/shard_map/all_gather | solution.py:49
  7.9 112.6 %all-gather.20.cloned.1.call-start = ((), (), s32[]{:S(2)}) async-start(), calls=%async_computation.8 | async-start | bytes 10027008 | tf_op jit(solution)/shard_map/all_gather | solution.py:59
  8.7 193.7 %all-gather.16.cloned.1.call-start = ((), (), s32[]{:S(2)}) async-start(), calls=%async_computation.6 | async-start | bytes 10027008 | tf_op jit(solution)/shard_map/all_gather | solution.py:62
  9.4 291.6 %all-gather.12.cloned.1.call-start = ((), (), s32[]{:S(2)}) async-start(), calls=%async_computation.4 | async-start | bytes 20054016 | tf_op jit(solution)/shard_map/all_gather | solution.py:56
  10.0 347.0 %all-gather.22.cloned.1.call-start = ((), (), s32[]{:S(2)}) async-start(), calls=%async_computation.9 | async-start | bytes 5013504 | tf_op jit(solution)/shard_map/all_gather | solution.py:76
  126.3 76.1 %copy-start.3 = (bf16[144,4608]{1,0:T(8,128)(2,1)S(1)}, bf16[144,4608]{1,0:T(8,128)(2,1)}, u32[]{:S(2)}) copy-start(bf16[144,4608]{1,0:T(8,128)(2,1)} %all-gather.10.cloned.1.call-done) | copy-start | bytes 3981316
  127.6 283.9 %all-gather.18.cloned.1.call-start = ((), (), s32[]{:S(2)}) async-start(), calls=%async_computation.7 | async-start | bytes 5013504 | tf_op jit(solution)/shard_map/all_gather | solution.py:77
  208.5 285.9 %all-gather.14.cloned.1.call-start = ((), (), s32[]{:S(2)}) async-start(), calls=%async_computation.5 | async-start | bytes 10027008 | tf_op jit(solution)/shard_map/all_gather | solution.py:75
  309.6 1.5 copy-start.9
  311.0 429.6 %reduce-scatter.10.cloned.1.call-start = ((), (), s32[]{:S(2)}) async-start(), calls=%async_computation.13 | async-start | bytes 626688
  424.1 1.4 copy-start.1
  424.1 3.1 copy-start
  629.0 211.3 %all-gather.24.cloned.1.call-start = ((), (), s32[]{:S(2)}) async-start(), calls=%async_computation.11 | async-start | bytes 20054016 | tf_op jit(solution)/shard_map/all_gather | solution.py:170
  629.7 326.4 %reduce-scatter.6.cloned.1.call-start = ((), (), s32[]{:S(2)}) async-start(), calls=%async_computation.10 | async-start | bytes 10027008 | tf_op jit(solution)/shard_map/reduce_scatter | solution.py:159
  629.8 0.7 copy-start.8
  630.3 361.0 %reduce-scatter.8.cloned.1.call-start = ((), (), s32[]{:S(2)}) async-start(), calls=%async_computation.12 | async-start | bytes 1990656 | tf_op jit(solution)/shard_map/reduce_scatter | solution.py:172
  956.5 11.5 %copy-start.5 = (bf16[2304]{0:T(1024)(128)(2,1)S(1)}, bf16[2304]{0:T(1024)(128)(2,1)}, u32[]{:S(2)}) copy-start(bf16[2304]{0:T(1024)(128)(2,1)} %param.26) | copy-start | bytes 13828
  968.0 29.5 %copy-start.2 = (bf16[144,2304]{1,0:T(8,128)(2,1)S(1)}, bf16[144,2304]{1,0:T(8,128)(2,1)}, u32[]{:S(2)}) copy-start(bf16[144,2304]{1,0:T(8,128)(2,1)} %param.20) | copy-start | bytes 1990660
Sparse Core Ops, SparseCore 0:
  9.6 27.1 all-gather.9
  39.0 81.4 all-gather.19
  122.8 79.5 all-gather.15
  203.9 97.0 all-gather.11
  303.7 53.2 all-gather.21
  359.7 51.7 all-gather.17
  414.3 79.9 all-gather.13
  629.1 111.4 reduce-scatter.9
  742.3 97.9 all-gather.23
  844.8 111.3 reduce-scatter.5
  968.2 23.0 reduce-scatter.7
where the time goes:
time: 1020 us; the launch traced here: 1010 us
  waiting for transfers between devices  778 us (76%)
  local copies, waits for them, and re-layouts  76.5 us (8%)
  matrix products  74.4 us (7%)
  loops' own time  33.8 us (3%)
  other arithmetic  18.7 us (2%)
  between operations  14.2 us (1%)
    reduce_scatter x1, waiting for transfers between devices, on_device(): lax.psum_scatter(numer_all.astype(jnp.bfloat16), 'gx', scatter_dimension=...  116 us
    unnamed x12, waiting for transfers between devices  114 us
    all_gather x1, waiting for transfers between devices, on_device(): lax.all_gather(w_o, 'gx', axis=1, tiled=True)  98.7 us
    all_gather x1, waiting for transfers between devices, on_device(): lax.all_gather(w_q, 'gx', axis=0, tiled=True)  92.4 us
    all_gather x1, waiting for transfers between devices, on_device(): lax.all_gather(w_k, 'gx', axis=0, tiled=True)  82.1 us
    all_gather x1, waiting for transfers between devices, on_device(): lax.all_gather(w_v, 'gx', axis=0, tiled=True)  74.8 us
    all_gather x1, waiting for transfers between devices, on_device(): lax.all_gather(q_new, 'gx', axis=0, tiled=True)  64.7 us
    all_gather x1, waiting for transfers between devices, on_device(): lax.all_gather(v_new, 'gx', axis=0, tiled=True)  46.4 us
  transfers between devices with their start and end apart: 11, of which 11 were waited for; matrix products, arithmetic and copies ran while one was open for 5% of the time, Pallas kernels for 0%

commit v1 on v0

v1 whole, which is shorter than its diff:
```python
import functools

import jax
import jax.numpy as jnp
from jax import lax
from jax.experimental import pallas as pl
from jax.experimental.pallas import tpu as pltpu
from jax.sharding import PartitionSpec as P

D = 4608
HD = 128
REQS = 12
NEWTOK = 192
KB = 256
VMEM_LIMIT = 56 * 1024 * 1024


epsilon = 1e-06
soft_cap = 50.0
query_scale = 144.0 ** (-0.5)


def project_kernel(q_blocks, rope_blocks, x_ref, w_ref, cos_ref, sin_ref, out_ref):
    block = pl.program_id(0)
    lin = jnp.dot(x_ref[...], w_ref[...], preferred_element_type=jnp.float32)
    heads = lin.shape[1] // HD

    @pl.when(block < rope_blocks)
    def _():
        scale = jnp.where(block < q_blocks, query_scale, 1.0)
        cosine = cos_ref[...] * scale
        sine = sin_ref[...] * scale
        for h in range(heads):
            u = lin[:, h * HD : (h + 1) * HD]
            swapped = pltpu.roll(u, HD // 2, 1)
            out_ref[:, h * HD : (h + 1) * HD] = (u * cosine + swapped * sine).astype(
                out_ref.dtype
            )

    @pl.when(block >= rope_blocks)
    def _():
        out_ref[...] = lin.astype(out_ref.dtype)


def project(normed, weights, cosine, sine, q_cols, rope_cols):
    rows, cols = normed.shape[0], weights.shape[1]
    width = min(512, cols - rope_cols)
    return pl.pallas_call(
        functools.partial(project_kernel, q_cols // width, rope_cols // width),
        grid=(cols // width,),
        in_specs=[
            pl.BlockSpec((rows, D), lambda i: (0, 0)),
            pl.BlockSpec((D, width), lambda i: (0, i)),
            pl.BlockSpec((rows, HD), lambda i: (0, 0)),
            pl.BlockSpec((rows, HD), lambda i: (0, 0)),
        ],
        out_specs=pl.BlockSpec((rows, width), lambda i: (0, i)),
        out_shape=jax.ShapeDtypeStruct((rows, cols), jnp.bfloat16),
        compiler_params=pltpu.CompilerParams(vmem_limit_bytes=VMEM_LIMIT),
        cost_estimate=pl.CostEstimate(
            flops=2 * rows * D * cols, bytes_accessed=2 * D * cols, transcendentals=0
        ),
    )(normed, weights, cosine, sine)


def attend_kernel(
    group, slab, info_ref, q_ref, k_ref, v_ref, kc_ref, vc_ref, kp_ref, vp_ref, nd_ref, acc_ref
):
    head = pl.program_id(0)
    gw = group * HD
    rows = group * NEWTOK
    den_at = nd_ref.shape[1] - HD
    kp_ref[...] = kc_ref[...]
    vp_ref[...] = vc_ref[...]
    num_cols = pl.ds(pl.multiple_of(head * gw, HD), gw)
    nd_ref[:, num_cols] = jnp.zeros((nd_ref.shape[0], gw), nd_ref.dtype)

    @pl.when(head == 0)
    def _():
        nd_ref[:, den_at:] = jnp.zeros((nd_ref.shape[0], HD), nd_ref.dtype)

    first = info_ref[3, 0]

    def request(r, carry):
        start = info_ref[2, r] - first
        cached = info_ref[0, r]
        fresh = info_ref[1, r]
        land = start + cached
        stop = land + fresh
        b_first = jnp.maximum(start, 0) // KB
        b_stop = (jnp.clip(stop, 0, slab) + (KB - 1)) // KB
        l_first = jnp.maximum(land, 0) // KB
        row0 = pl.multiple_of(r * NEWTOK, NEWTOK)

        @pl.when(b_stop > b_first)
        def _():
            def write(j, c):
                base = pl.multiple_of(j * KB, KB)
                at = lax.broadcasted_iota(jnp.int32, (KB, NEWTOK), 0) + (base - land)
                col = lax.broadcasted_iota(jnp.int32, (KB, NEWTOK), 1)
                pick = jnp.where((at == col) & (col < fresh), 1.0, 0.0).astype(jnp.bfloat16)
                here = lax.broadcasted_iota(jnp.int32, (KB, HD), 0) + (base - land)
                new = (here >= 0) & (here < fresh)
                for src, dst in ((k_ref, kp_ref), (v_ref, vp_ref)):
                    got = jnp.dot(
                        pick, src[pl.ds(row0, NEWTOK), :], preferred_element_type=jnp.float32
                    )
                    old = dst[pl.ds(base, KB), :].astype(jnp.float32)
                    dst[pl.ds(base, KB), :] = jnp.where(new, got, old).astype(dst.dtype)
                return c

            lax.fori_loop(l_first, b_stop, write, 0)

            acc_ref[...] = jnp.zeros_like(acc_ref)
            q = jnp.concatenate(
                [q_ref[pl.ds(row0, NEWTOK), g * HD : (g + 1) * HD] for g in range(group)], axis=0
            )
            ones = jnp.ones((KB, HD), jnp.bfloat16)
            index = lax.broadcasted_iota(jnp.int32, (rows, KB), 0) % NEWTOK
            last = cached + jnp.minimum(index, fresh - 1)
            slot = lax.broadcasted_iota(jnp.int32, (rows, KB), 1)

            def block(j, c):
                base = pl.multiple_of(j * KB, KB)
                logits = lax.dot_general(
                    q,
                    kp_ref[pl.ds(base, KB), :],
                    (((1,), (1,)), ((), ())),
                    preferred_element_type=jnp.float32,
                )
                weight = jnp.exp(soft_cap * jnp.tanh(logits * (1.0 / soft_cap)))
                at = slot + (base - start)
                weight = jnp.where((at >= 0) & (at <= last), weight, 0.0).astype(jnp.bfloat16)
                values = jnp.concatenate([vp_ref[pl.ds(base, KB), :], ones], axis=1)
                acc_ref[...] += jnp.dot(weight, values, preferred_element_type=jnp.float32)
                return c

            lax.fori_loop(b_first, b_stop, block, 0)
            for g in range(group):
                nd_ref[
                    pl.ds(row0, NEWTOK), pl.ds(pl.multiple_of(head * gw + g * HD, HD), HD)
                ] = acc_ref[g * NEWTOK : (g + 1) * NEWTOK, :HD].astype(nd_ref.dtype)
            lane = lax.broadcasted_iota(jnp.int32, (NEWTOK, HD), 1)
            den = nd_ref[pl.ds(row0, NEWTOK), den_at:].astype(jnp.float32)
            for g in range(group):
                den = jnp.where(
                    lane == head * group + g, acc_ref[g * NEWTOK : (g + 1) * NEWTOK, HD:], den
                )
            nd_ref[pl.ds(row0, NEWTOK), den_at:] = den.astype(nd_ref.dtype)

        return carry

    lax.fori_loop(0, REQS, request, 0)


def attend(info, qkv, k_cache, v_cache):
    slab, kv_cols = k_cache.shape
    total = qkv.shape[0]
    kv = kv_cols // HD
    q_cols = qkv.shape[1] - 2 * kv_cols
    group = q_cols // kv_cols
    pool = pl.BlockSpec((slab, HD), lambda c: (0, c))
    return pl.pallas_call(
        functools.partial(attend_kernel, group, slab),
        grid=(kv,),
        in_specs=[
            pl.BlockSpec(memory_space=pltpu.SMEM),
            pl.BlockSpec((total, group * HD), lambda c: (0, c)),
            pl.BlockSpec((total, HD), lambda c: (0, q_cols // HD + c)),
            pl.BlockSpec((total, HD), lambda c: (0, (q_cols + kv_cols) // HD + c)),
            pool,
            pool,
        ],
        out_specs=[
            pool,
            pool,
            pl.BlockSpec((total, q_cols + HD), lambda c: (0, 0)),
        ],
        out_shape=[
            jax.ShapeDtypeStruct(k_cache.shape, k_cache.dtype),
            jax.ShapeDtypeStruct(v_cache.shape, v_cache.dtype),
            jax.ShapeDtypeStruct((total, q_cols + HD), jnp.bfloat16),
        ],
        scratch_shapes=[pltpu.VMEM((group * NEWTOK, 2 * HD), jnp.float32)],
        compiler_params=pltpu.CompilerParams(vmem_limit_bytes=VMEM_LIMIT),
        cost_estimate=pl.CostEstimate(
            flops=4 * 2 * NEWTOK * slab * q_cols * 2,
            bytes_accessed=2 * total * (2 * q_cols + 2 * kv_cols),
            transcendentals=4 * NEWTOK * slab * q_cols // HD,
        ),
    )(info, qkv, qkv, qkv, k_cache, v_cache)


def on_device(
    tokens,
    pre_gain,
    w_q,
    w_k,
    w_v,
    w_o,
    post_gain,
    k_cache,
    v_cache,
    cached_len,
    new_len,
    slot_offset,
):
    tok_rows = tokens.shape[0]
    q_cols, kv_cols = w_q.shape[1], w_k.shape[1]
    n_gy = D // tokens.shape[1]
    gy = lax.axis_index("gy")
    weights = lax.all_gather(jnp.concatenate([w_q, w_k, w_v], axis=1), "gx", axis=0, tiled=True)
    if n_gy == 2:
        swap = [(0, 1), (1, 0)]
        other_in = lax.ppermute(tokens, "gy", swap)
        other_gain = lax.ppermute(pre_gain, "gy", swap)
        whole_in = jnp.where(
            gy == 0,
            jnp.concatenate([tokens, other_in], axis=1),
            jnp.concatenate([other_in, tokens], axis=1),
        )
        whole_gain = jnp.where(
            gy == 0,
            jnp.concatenate([pre_gain, other_gain]),
            jnp.concatenate([other_gain, pre_gain]),
        )
    else:
        whole_in = lax.all_gather(tokens, "gy", axis=1, tiled=True)
        whole_gain = lax.all_gather(pre_gain, "gy", axis=0, tiled=True)
    float_in = whole_in.astype(jnp.float32)
    scale_rows = lax.rsqrt(jnp.mean(float_in * float_in, axis=1, keepdims=True) + epsilon)
    normed = (float_in * scale_rows * (1.0 + whole_gain.astype(jnp.float32))).astype(jnp.bfloat16)
    row_ids = lax.axis_index("gx") * tok_rows + jnp.arange(tok_rows, dtype=jnp.int32)
    request = row_ids // NEWTOK
    within = row_ids % NEWTOK
    owner_mask = request[:, None] == jnp.arange(REQS, dtype=jnp.int32)[None, :]
    row_cached = jnp.sum(jnp.where(owner_mask, cached_len[None, :], 0), axis=1)
    row_fresh = jnp.sum(jnp.where(owner_mask, new_len[None, :], 0), axis=1)
    position = row_cached + within
    half = HD // 2
    inverse = jnp.power(10000.0, -2.0 * jnp.arange(half, dtype=jnp.float32) / HD)
    angle = position.astype(jnp.float32)[:, None] * inverse[None, :]
    cosine, sine = jnp.cos(angle), jnp.sin(angle)
    cosine = jnp.concatenate([cosine, cosine], axis=1)
    sine = jnp.concatenate([-sine, sine], axis=1)
    qkv_new = project(normed, weights, cosine, sine, q_cols, q_cols + kv_cols)
    qkv = lax.all_gather(qkv_new, "gx", axis=0, tiled=True)
    qkv, w_o = lax.optimization_barrier((qkv, w_o))
    w_out = lax.all_gather(w_o, "gx", axis=1, tiled=True)
    slab = k_cache.shape[0]
    first = jnp.full((REQS,), lax.axis_index("gx") * slab, jnp.int32)
    info = jnp.stack([cached_len, new_len, slot_offset, first])
    k_pool, v_pool, num_den = attend(info, qkv, k_cache, v_cache)
    sums = lax.psum_scatter(num_den, "gx", scatter_dimension=0, tiled=True).astype(jnp.float32)
    heads = q_cols // HD
    head_num = sums[:, :q_cols].reshape(tok_rows, heads, HD)
    head_den = sums[:, q_cols : q_cols + heads]
    attended = head_num / head_den[:, :, None]
    attended = jnp.where((within < row_fresh)[:, None, None], attended, 0.0)
    attended = attended.reshape(tok_rows, q_cols).astype(jnp.bfloat16)
    partial_out = jnp.dot(attended, w_out, preferred_element_type=jnp.float32).astype(jnp.bfloat16)
    if n_gy == 2:
        low, high = partial_out[:, : D // 2], partial_out[:, D // 2 :]
        theirs = lax.ppermute(jnp.where(gy == 0, high, low), "gy", swap)
        branch = jnp.where(gy == 0, low, high).astype(jnp.float32) + theirs.astype(jnp.float32)
        square = jnp.sum(branch * branch, axis=1)
        mean_square = (square + lax.ppermute(square, "gy", swap)) / D
    else:
        branch = lax.psum_scatter(partial_out, "gy", scatter_dimension=1, tiled=True).astype(
            jnp.float32
        )
        mean_square = lax.psum(jnp.sum(branch * branch, axis=1), "gy") / D
    layer_out = (
        tokens.astype(jnp.float32)
        + branch * lax.rsqrt(mean_square + epsilon)[:, None] * (1.0 + post_gain.astype(jnp.float32))
    ).astype(jnp.bfloat16)
    return (layer_out, k_pool, v_pool)


def solution(mesh):
    placed = (
        P("gx", "gy"),
        P("gy"),
        P("gx", "gy"),
        P("gx", "gy"),
        P("gx", "gy"),
        P("gy", "gx"),
        P("gy"),
        P("gx", "gy"),
        P("gx", "gy"),
        P(),
        P(),
        P(),
    )
    return jax.shard_map(
        on_device,
        mesh=mesh,
        in_specs=placed,
        out_specs=(P("gx", "gy"), P("gx", "gy"), P("gx", "gy")),
        check_vma=False,
    )
```

time: 1020 us -> 614 us (0.60); the launches traced: 1010 us -> 613 us
  waiting for transfers between devices: 778 us -> 514 us
  local copies, waits for them, and re-layouts: 76.5 us -> 2.23 us
  matrix products: 74.4 us -> 10.7 us
  Pallas kernels: 0 us -> 55.8 us
  loops' own time: 33.8 us -> 0 us
    all_gather x8 -> x3, waiting for transfers between devices: 525 us -> 365 us  [the longest x1 170 us: on_device(): lax.all_gather(jnp.concatenate([w_q, w_k, w_v], axis=1), 'gx', axis=0, ti...]
    unnamed x12 -> x4, waiting for transfers between devices: 114 us -> 0.57 us
    dot_general x12 -> x1, matrix products: 74.4 us -> 10.7 us  [on_device(): jnp.dot(attended, w_out, preferred_element_type=jnp.float32)]
    pallas_call x0 -> x2, Pallas kernels: none -> 55.8 us  [the longest x1 39.1 us: attend(): pl.pallas_call(functools.partial(attend_kernel, group, slab), grid=(kv,),...]
    another operation x15 -> x0, loops' own time: 33.8 us -> none  [the longest x1 31.9 us: on_device(): numer_all, denom_all = lax.fori_loop(0, REQS, request_step, start_sums)]
    ppermute x0 -> x4, waiting for transfers between devices: none -> 31.4 us  [the longest x1 15.6 us: on_device(): theirs = lax.ppermute(jnp.where(gy == 0, high, low), 'gy', swap)]
    dynamic_slice x38 -> x0, local copies, waits for them, and re-layouts: 24.4 us -> none  [the longest x12 7.72 us: request_step(): fresh_count = new_len[request_id]]
    reduce_scatter x2 -> x1, waiting for transfers between devices: 139 us -> 117 us  [on_device(): lax.psum_scatter(num_den, 'gx', scatter_dimension=0, tiled=True)]
  transfers between devices with their start and end apart: 11 -> 8, of which waited for: 11 -> 7; matrix products, arithmetic and copies ran while one was open for 5% -> 1% of each run, Pallas kernels for 0% -> 0%
where the time goes in v1:
time: 614 us; the launch traced here: 613 us
  waiting for transfers between devices  514 us (84%)
  Pallas kernels  55.8 us (9%)
  between operations  13.9 us (2%)
  matrix products  10.7 us (2%)
  other arithmetic  10.2 us (2%)
  starting transfers between devices  6.24 us (1%)
    all_gather x1, waiting for transfers between devices, on_device(): lax.all_gather(jnp.concatenate([w_q, w_k, w_v], axis=1), 'gx', axis=0, ti...  170 us
    reduce_scatter x1, waiting for transfers between devices, on_device(): lax.psum_scatter(num_den, 'gx', scatter_dimension=0, tiled=True)  117 us
    all_gather x1, waiting for transfers between devices, on_device(): qkv = lax.all_gather(qkv_new, 'gx', axis=0, tiled=True)  98.3 us
    all_gather x1, waiting for transfers between devices, on_device(): w_out = lax.all_gather(w_o, 'gx', axis=1, tiled=True)  97.6 us
    pallas_call x1, Pallas kernels, attend(): pl.pallas_call(functools.partial(attend_kernel, group, slab), grid=(kv,),...  39.1 us
    pallas_call x1, Pallas kernels, project(): pl.pallas_call(functools.partial(project_kernel, q_cols // width, rope_co...  16.7 us
    ppermute x1, waiting for transfers between devices, on_device(): theirs = lax.ppermute(jnp.where(gy == 0, high, low), 'gy', swap)  15.6 us
    ppermute x1, waiting for transfers between devices, on_device(): other_gain = lax.ppermute(pre_gain, 'gy', swap)  13.7 us
  transfers between devices with their start and end apart: 8, of which 7 were waited for; matrix products, arithmetic and copies ran while one was open for 1% of the time, Pallas kernels for 0%

profile of v1, /device:TPU:0, one launch (start us, length us, event | category | flops | bytes accessed | tf_op | source)
XLA Modules:
  0.0 613.1 jit_solution(13890225533258143382)
XLA Ops:
  7.2 0.0 all-gather.4.cloned.1.call-start
  7.2 3.3 pad_maximum_fusion
  10.5 0.0 copy-start
  10.5 0.0 copy-start.1
  10.5 0.0 copy-start.3
  10.5 0.0 copy-start.4
  10.5 0.0 all-gather.4.cloned.1.call-update
  10.5 0.0 all-gather.6.cloned.1.call-start
  10.6 1.0 copy-done
  11.6 3.0 collective-permute-start
  14.5 0.0 copy-done.1
  14.5 0.0 collective-permute-start.1
  14.6 0.0 copy-done.3
  14.6 0.0 copy-done.4
  14.6 0.1 select_reduce_fusion.1
  14.7 0.3 fusion.8
  15.1 0.8 pad_maximum_fusion.1
  15.8 13.7 %collective-permute-done.1 = bf16[2304]{0:T(1024)(128)(2,1)S(1)} collective-permute-done((bf16[2304]{0:T(1024)(128)(2,1)S(1)}, bf16[2304]{0:T(1024)(128)(2,1)S(1)}, u32[]{:S(2)}, u32[]{:S(2)}) %collective-permute-start.1) | collective-permute-done | bytes 4640 | tf_op jit(solution)/shard_map/ppermute | solution.py:216
  29.6 0.0 collective-permute-done
  29.6 0.5 fusion
  30.1 1.6 fusion.2.x_ref
  31.6 169.5 %all-gather.4.cloned.1.call-done.w_ref = bf16[4608,4096]{1,0:T(8,128)(2,1)} async-done(((bf16[288,4096]{1,0:T(8,128)(2,1)}), bf16[4608,4096]{1,0:T(8,128)(2,1)}) %all-gather.4.cloned.1.call-update) | async-done | bytes 37748752 | tf_op jit(solution)/shard_map/all_gather | solution.py:212
  201.2 0.0 copy-start.5
  201.2 16.7 %shard_map.139 = bf16[144,4096]{1,0:T(8,128)(2,1)} custom-call(bf16[144,4608]{1,0:T(8,128)(2,1)} %fusion.2.x_ref, bf16[4608,4096]{1,0:T(8,128)(2,1)} %all-gather.4.cloned.1.call-done.w_ref, f32[144,128]{1,0:T(8,128)} %get-tuple-element.18.cos_ref, f32[144,128]{1,0:T(8,128)} %get-tuple-element.19.sin_ref), custom_call_target="tpu_custom_call" | custom-call | flops 5435817984 | bytes 37748736 | tf_op jit(solution)/shard_map/pallas_call | solution.py:48
  217.9 0.0 all-gather.6.cloned.1.call-update
  217.9 0.0 reduce-scatter.2.cloned.1.call-start
  218.0 0.1 pad.18.clone
  218.0 0.0 copy-done.5
  218.0 0.6 add_add_fusion.info_ref
  218.7 98.3 %all-gather.6.cloned.1.call-done.q_ref.k_ref.v_ref = bf16[2304,4096]{1,0:T(8,128)(2,1)} async-done(((bf16[144,4096]{1,0:T(8,128)(2,1)}), bf16[2304,4096]{1,0:T(8,128)(2,1)}) %all-gather.6.cloned.1.call-update) | async-done | bytes 18874384 | tf_op jit(solution)/shard_map/all_gather | solution.py:247
  317.0 39.1 %shard_map.140 = (bf16[1024,1024]{1,0:T(8,128)(2,1)}, bf16[1024,1024]{1,0:T(8,128)(2,1)}, bf16[2304,2176]{1,0:T(8,128)(2,1)}) custom-call(s32[4,12]{1,0:T(4,128)} %add_add_fusion.info_ref, bf16[2304,4096]{1,0:T(8,128)(2,1)} %all-gather.6.cloned.1.call-done.q_ref.k_ref.v_ref, bf16[2304,4096]{1,0:T(8,128)(2,1)} %all-gather.6.cloned.1.call-done.q_ref.k_ref.v_ref, ...), custom_call_target="tpu_custom_call" | custom-call | flops 6442450944 | bytes 28311552 | tf_op jit(solution)/shard_map/pallas_call | solution.py:163
  356.1 0.0 reduce-scatter.2.cloned.1.call-update
  356.2 0.0 all-gather.8.cloned.1.call-start
  356.2 0.5 all-gather.8.cloned.1.call-update
  356.8 116.6 %reduce-scatter.2.cloned.1.call-done = bf16[144,2176]{1,0:T(8,128)(2,1)} async-done(((bf16[2304,2176]{1,0:T(8,128)(2,1)}), bf16[144,2176]{1,0:T(8,128)(2,1)}) %reduce-scatter.2.cloned.1.call-update) | async-done | bytes 626704 | tf_op jit(solution)/shard_map/reduce_scatter | solution.py:254
  473.4 0.8 slice.17
  474.1 1.2 convert_element_type.49
  475.3 97.6 %all-gather.8.cloned.1.call-done = bf16[2048,4608]{0,1:T(8,128)(2,1)} async-done(((bf16[2048,288]{0,1:T(8,128)(2,1)}), bf16[2048,4608]{0,1:T(8,128)(2,1)}) %all-gather.8.cloned.1.call-update) | async-done | bytes 18874384 | tf_op jit(solution)/shard_map/all_gather | solution.py:249
  572.9 0.4 div.42
  573.3 10.7 %convolution_convert_fusion = bf16[144,4608]{1,0:T(8,128)(2,1)S(1)} fusion(bf16[2048,4608]{0,1:T(8,128)(2,1)} %all-gather.8.cloned.1.call-done, f32[18,8,16,128]{3,2,1,0:T(8,128)S(1)} %bitcast.13, f32[144,2176]{1,0:T(8,128)S(1)} %convert_element_type.49, pred[144]{0:T(512)(128)(4,1)S(1)} %fusion.11), kind=kOutput, calls=%fused_computation | convolution fusion | flops 2719457280 | bytes 22561280 | tf_op jit(solution)/shard_map/dot_general | solution.py:261
  584.0 0.1 broadcast_select_fusion
  584.0 0.0 copy-start.2
  584.0 1.5 collective-permute-start.2
  585.6 15.6 %collective-permute-done.2 = bf16[144,2304]{1,0:T(8,128)(2,1)S(1)} collective-permute-done((bf16[144,2304]{1,0:T(8,128)(2,1)S(1)}, bf16[144,2304]{1,0:T(8,128)(2,1)S(1)}, u32[]{:S(2)}, u32[]{:S(2)}) %collective-permute-start.2) | collective-permute-done | bytes 663584 | tf_op jit(solution)/shard_map/ppermute | solution.py:264
  601.2 0.4 multiply_reduce_fusion
  601.6 1.5 collective-permute-start.3
  603.1 0.0 copy-done.2
  603.1 2.1 collective-permute-done.3
  605.2 1.3 add_convert_fusion
  (8 shorter events, 0.1 us)
Async XLA Ops:
  7.2 194.0 %all-gather.4.cloned.1.call-start = ((), (), s32[]{:S(2)}) async-start(), calls=%async_computation.1 | async-start | bytes 40108032 | tf_op jit(solution)/shard_map/all_gather | solution.py:212
  10.5 1.1 copy-start
  10.5 4.1 copy-start.1
  10.5 4.1 copy-start.3
  10.5 4.1 copy-start.4
  10.5 306.5 %all-gather.6.cloned.1.call-start = ((), (), s32[]{:S(2)}) async-start(), calls=%async_computation.2 | async-start | bytes 20054016 | tf_op jit(solution)/shard_map/all_gather | solution.py:247
  11.6 18.0 %collective-permute-start = (bf16[144,2304]{1,0:T(8,128)(2,1)S(1)}, bf16[144,2304]{1,0:T(8,128)(2,1)S(1)}, u32[]{:S(2)}, u32[]{:S(2)}) collective-permute-start(bf16[144,2304]{1,0:T(8,128)(2,1)S(1)} %copy-done), channel_id=1, source_target_pairs={{0,1},{1,0},{2,3},{3,2},{4,5},{5,4},{6,7},{7,6},{8,9},{9,8},{10,11... | collective-permute-start | bytes 1990664 | tf_op jit(solution)/shard_map/ppermute | solution.py:215
  14.5 15.0 %collective-permute-start.1 = (bf16[2304]{0:T(1024)(128)(2,1)S(1)}, bf16[2304]{0:T(1024)(128)(2,1)S(1)}, u32[]{:S(2)}, u32[]{:S(2)}) collective-permute-start(bf16[2304]{0:T(1024)(128)(2,1)S(1)} %copy-done.1), channel_id=1, source_target_pairs={{0,1},{1,0},{2,3},{3,2},{4,5},{5,4},{6,7},{7,6},{8,9},{9,8},{10,11... | collective-permute-start | bytes 13832 | tf_op jit(solution)/shard_map/ppermute | solution.py:216
  201.2 16.9 %copy-start.5 = (s32[12]{0:T(128)S(1)}, s32[12]{0:T(128)}, u32[]{:S(2)}) copy-start(s32[12]{0:T(128)} %param.23) | copy-start | bytes 148
  217.9 255.4 %reduce-scatter.2.cloned.1.call-start = ((), (), s32[]{:S(2)}) async-start(), calls=%async_computation.3 | async-start | bytes 10653696 | tf_op jit(solution)/shard_map/reduce_scatter | solution.py:254
  356.2 216.7 %all-gather.8.cloned.1.call-start = ((), (), s32[]{:S(2)}) async-start(), calls=%async_computation.4 | async-start | bytes 20054016 | tf_op jit(solution)/shard_map/all_gather | solution.py:249
  584.0 19.1 %copy-start.2 = (bf16[2304]{0:T(1024)(128)(2,1)S(1)}, bf16[2304]{0:T(1024)(128)(2,1)}, u32[]{:S(2)}) copy-start(bf16[2304]{0:T(1024)(128)(2,1)} %param.18) | copy-start | bytes 13828
  584.0 17.1 %collective-permute-start.2 = (bf16[144,2304]{1,0:T(8,128)(2,1)S(1)}, bf16[144,2304]{1,0:T(8,128)(2,1)S(1)}, u32[]{:S(2)}, u32[]{:S(2)}) collective-permute-start(bf16[144,2304]{1,0:T(8,128)(2,1)S(1)} %broadcast_select_fusion), channel_id=1, source_target_pairs={{0,1},{1,0},{2,3},{3,2},{4,5},{5,4},{6,7},{7,6},{8,9},{9,8},{10,11... | collective-permute-start | bytes 1990664 | tf_op jit(solution)/shard_map/ppermute | solution.py:264
  601.6 3.6 collective-permute-start.3
Sparse Core Ops, SparseCore 0:
  10.6 190.5 all-gather.3
  218.0 98.9 all-gather.5
  356.3 117.0 reduce-scatter.1
  474.8 98.0 all-gather.7

commit v2 on v1

--- a/solution.py
+++ b/solution.py
@@ -189,6 +189,36 @@
             transcendentals=4 * NEWTOK * slab * q_cols // HD,
         ),
     )(info, qkv, qkv, qkv, k_cache, v_cache)
+
+
+def out_kernel(half_ref, x_ref, w_ref, out_ref):
+    out_ref[...] = lax.dot_general(
+        x_ref[...], w_ref[...], (((1,), (1,)), ((), ())), preferred_element_type=jnp.float32
+    ).astype(out_ref.dtype)
+
+
+def out_half(attended, w_out, half):
+    rows, depth = attended.shape
+    cols = w_out.shape[0] // 2
+    width = 384
+    steps = cols // width
+    return pl.pallas_call(
+        out_kernel,
+        grid_spec=pltpu.PrefetchScalarGridSpec(
+            num_scalar_prefetch=1,
+            grid=(steps,),
+            in_specs=[
+                pl.BlockSpec((rows, depth), lambda i, half: (0, 0)),
+                pl.BlockSpec((width, depth), lambda i, half: (half[0] * steps + i, 0)),
+            ],
+            out_specs=pl.BlockSpec((rows, width), lambda i, half: (0, i)),
+        ),
+        out_shape=jax.ShapeDtypeStruct((rows, cols), jnp.bfloat16),
+        compiler_params=pltpu.CompilerParams(vmem_limit_bytes=VMEM_LIMIT),
+        cost_estimate=pl.CostEstimate(
+            flops=2 * rows * depth * cols, bytes_accessed=2 * depth * cols, transcendentals=0
+        ),
+    )(half.reshape(1).astype(jnp.int32), attended, w_out)
 
 
 def on_device(
@@ -245,27 +275,43 @@
     sine = jnp.concatenate([-sine, sine], axis=1)
     qkv_new = project(normed, weights, cosine, sine, q_cols, q_cols + kv_cols)
     qkv = lax.all_gather(qkv_new, "gx", axis=0, tiled=True)
-    qkv, w_o = lax.optimization_barrier((qkv, w_o))
-    w_out = lax.all_gather(w_o, "gx", axis=1, tiled=True)
+    qkv, w_o_t = lax.optimization_barrier((qkv, w_o.T))
+    w_out = lax.all_gather(w_o_t, "gx", axis=0, tiled=True)
     slab = k_cache.shape[0]
     first = jnp.full((REQS,), lax.axis_index("gx") * slab, jnp.int32)
     info = jnp.stack([cached_len, new_len, slot_offset, first])
     k_pool, v_pool, num_den = attend(info, qkv, k_cache, v_cache)
-    sums = lax.psum_scatter(num_den, "gx", scatter_dimension=0, tiled=True).astype(jnp.float32)
+    n_gx = num_den.shape[0] // tok_rows
+    core = lax.axis_index("gx") % 2
+    halves = num_den.reshape(n_gx // 2, 2, tok_rows, num_den.shape[1])
+    kept = jnp.where(core == 0, halves[:, 0], halves[:, 1])
+    given = jnp.where(core == 0, halves[:, 1], halves[:, 0])
+    taken = lax.ppermute(given, "gx", [(i, i ^ 1) for i in range(n_gx)])
+    chip = (kept.astype(jnp.float32) + taken.astype(jnp.float32)).astype(jnp.bfloat16)
+    chip, w_out = lax.optimization_barrier((chip, w_out))
+    sums = lax.psum_scatter(
+        chip.reshape(n_gx // 2 * tok_rows, num_den.shape[1]),
+        "gx",
+        scatter_dimension=0,
+        axis_index_groups=[list(range(c, n_gx, 2)) for c in range(2)],
+        tiled=True,
+    ).astype(jnp.float32)
     heads = q_cols // HD
     head_num = sums[:, :q_cols].reshape(tok_rows, heads, HD)
     head_den = sums[:, q_cols : q_cols + heads]
     attended = head_num / head_den[:, :, None]
     attended = jnp.where((within < row_fresh)[:, None, None], attended, 0.0)
     attended = attended.reshape(tok_rows, q_cols).astype(jnp.bfloat16)
-    partial_out = jnp.dot(attended, w_out, preferred_element_type=jnp.float32).astype(jnp.bfloat16)
     if n_gy == 2:
-        low, high = partial_out[:, : D // 2], partial_out[:, D // 2 :]
-        theirs = lax.ppermute(jnp.where(gy == 0, high, low), "gy", swap)
-        branch = jnp.where(gy == 0, low, high).astype(jnp.float32) + theirs.astype(jnp.float32)
+        theirs = lax.ppermute(out_half(attended, w_out, 1 - gy), "gy", swap)
+        own = out_half(attended, w_out, gy)
+        branch = own.astype(jnp.float32) + theirs.astype(jnp.float32)
         square = jnp.sum(branch * branch, axis=1)
         mean_square = (square + lax.ppermute(square, "gy", swap)) / D
     else:
+        partial_out = lax.dot_general(
+            attended, w_out, (((1,), (1,)), ((), ())), preferred_element_type=jnp.float32
+        ).astype(jnp.bfloat16)
         branch = lax.psum_scatter(partial_out, "gy", scatter_dimension=1, tiled=True).astype(
             jnp.float32
         )

time: 614 us -> 563 us (0.917)
  waiting for transfers between devices: 514 us -> 456 us
  other arithmetic: 10.2 us -> 27.8 us
  matrix products: 10.7 us -> 0 us
    all_gather x1, waiting for transfers between devices: 97.6 us -> 52.5 us  [on_device(): w_out = lax.all_gather(w_o_t, 'gx', axis=0, tiled=True)]
    pallas_call x0 -> x2, Pallas kernels: none -> 15.7 us  [out_half(): pl.pallas_call(out_kernel, grid_spec=pltpu.PrefetchScalarGridSpec(num_sca...]
    pallas_call x1, Pallas kernels: 39.1 us -> 24 us  [attend(): pl.pallas_call(functools.partial(attend_kernel, group, slab), grid=(kv,),...]
    ppermute x1, waiting for transfers between devices: 0.01 us -> 14.7 us  [on_device(): other_in = lax.ppermute(tokens, 'gy', swap)]
    ppermute x1, waiting for transfers between devices: 13.7 us -> 0.01 us  [on_device(): other_gain = lax.ppermute(pre_gain, 'gy', swap)]
    reduce_scatter x1, waiting for transfers between devices: 117 us -> 103 us  [on_device(): lax.psum_scatter(chip.reshape(n_gx // 2 * tok_rows, num_den.shape[1]), 'g...]
    convert_element_type x1 -> x3, other arithmetic: 1.16 us -> 12.2 us  [the longest x1 9.77 us: on_device(): (kept.astype(jnp.float32) + taken.astype(jnp.float32)).astype(jnp.bfloat16)]
    dot_general x1 -> x0, matrix products: 10.7 us -> none  [on_device(): jnp.dot(attended, w_out, preferred_element_type=jnp.float32)]
  transfers between devices with their start and end apart: 8 -> 9, of which waited for: 7 -> 8; matrix products, arithmetic and copies ran while one was open for 1% -> 3% of each run, Pallas kernels for 0% -> 6%
where the time goes in v2:
time: 563 us; the launch traced here: 562 us
  waiting for transfers between devices  456 us (81%)
  Pallas kernels  56.4 us (10%)
  other arithmetic  27.8 us (5%)
  between operations  13.8 us (2%)
  starting transfers between devices  6.9 us (1%)
    all_gather x1, waiting for transfers between devices, on_device(): lax.all_gather(jnp.concatenate([w_q, w_k, w_v], axis=1), 'gx', axis=0, ti...  169 us
    reduce_scatter x1, waiting for transfers between devices, on_device(): lax.psum_scatter(chip.reshape(n_gx // 2 * tok_rows, num_den.shape[1]), 'g...  103 us
    all_gather x1, waiting for transfers between devices, on_device(): qkv = lax.all_gather(qkv_new, 'gx', axis=0, tiled=True)  99.1 us
    all_gather x1, waiting for transfers between devices, on_device(): w_out = lax.all_gather(w_o_t, 'gx', axis=0, tiled=True)  52.5 us
    pallas_call x1, Pallas kernels, attend(): pl.pallas_call(functools.partial(attend_kernel, group, slab), grid=(kv,),...  24 us
    pallas_call x1, Pallas kernels, project(): pl.pallas_call(functools.partial(project_kernel, q_cols // width, rope_co...  16.7 us
    pallas_call x2, Pallas kernels, out_half(): pl.pallas_call(out_kernel, grid_spec=pltpu.PrefetchScalarGridSpec(num_sca...  15.7 us
    ppermute x1, waiting for transfers between devices, on_device(): other_in = lax.ppermute(tokens, 'gy', swap)  14.7 us
  transfers between devices with their start and end apart: 9, of which 8 were waited for; matrix products, arithmetic and copies ran while one was open for 3% of the time, Pallas kernels for 6%

profile of v2, /device:TPU:0, one launch (start us, length us, event | category | flops | bytes accessed | tf_op | source)
XLA Modules:
  0.0 562.4 jit_solution(17174457893169834654)
XLA Ops:
  7.2 0.0 all-gather.4.cloned.1.call-start
  7.2 3.3 pad_maximum_fusion
  10.5 0.0 copy-start.1
  10.5 0.0 copy-start
  10.5 0.0 copy-start.3
  10.5 0.0 copy-start.4
  10.5 0.0 all-gather.4.cloned.1.call-update
  10.5 0.0 all-gather.6.cloned.1.call-start
  10.6 0.6 copy-done.1
  11.2 3.0 collective-permute-start.1
  14.1 0.0 copy-done
  14.1 0.4 collective-permute-start
  14.6 0.0 copy-done.3
  14.6 0.0 copy-done.4
  14.6 0.1 select_reduce_fusion.1
  14.7 0.3 fusion.6
  15.0 0.8 pad_maximum_fusion.1
  15.8 0.0 collective-permute-done.1
  15.8 14.7 %collective-permute-done = bf16[144,2304]{1,0:T(8,128)(2,1)S(1)} collective-permute-done((bf16[144,2304]{1,0:T(8,128)(2,1)S(1)}, bf16[144,2304]{1,0:T(8,128)(2,1)S(1)}, u32[]{:S(2)}, u32[]{:S(2)}) %collective-permute-start) | collective-permute-done | bytes 663584 | tf_op jit(solution)/shard_map/ppermute | solution.py:245
  30.5 0.5 fusion.1
  31.0 1.6 fusion.3.x_ref
  32.5 168.6 %all-gather.4.cloned.1.call-done.w_ref = bf16[4608,4096]{1,0:T(8,128)(2,1)} async-done(((bf16[288,4096]{1,0:T(8,128)(2,1)}), bf16[4608,4096]{1,0:T(8,128)(2,1)}) %all-gather.4.cloned.1.call-update) | async-done | bytes 37748752 | tf_op jit(solution)/shard_map/all_gather | solution.py:242
  201.2 16.7 %shard_map.139 = bf16[144,4096]{1,0:T(8,128)(2,1)} custom-call(bf16[144,4608]{1,0:T(8,128)(2,1)} %fusion.3.x_ref, bf16[4608,4096]{1,0:T(8,128)(2,1)} %all-gather.4.cloned.1.call-done.w_ref, f32[144,128]{1,0:T(8,128)} %get-tuple-element.22.cos_ref, f32[144,128]{1,0:T(8,128)} %get-tuple-element.23.sin_ref), custom_call_target="tpu_custom_call" | custom-call | flops 5435817984 | bytes 37748736 | tf_op jit(solution)/shard_map/pallas_call | solution.py:48
  217.9 0.0 copy-start.5
  217.9 0.0 all-gather.6.cloned.1.call-update
  217.9 0.0 all-gather.8.cloned.1.call-start
  217.9 99.1 %all-gather.6.cloned.1.call-done.q_ref.k_ref.v_ref = bf16[2304,4096]{1,0:T(8,128)(2,1)} async-done(((bf16[144,4096]{1,0:T(8,128)(2,1)}), bf16[2304,4096]{1,0:T(8,128)(2,1)}) %all-gather.6.cloned.1.call-update) | async-done | bytes 18874384 | tf_op jit(solution)/shard_map/all_gather | solution.py:277
  317.0 0.0 all-gather.8.cloned.1.call-update
  317.0 0.0 reduce-scatter.2.cloned.1.call-start
  317.1 0.1 pad.18.clone
  317.2 0.0 copy-done.5
  317.2 0.6 add_add_fusion.info_ref
  317.8 24.0 %shard_map.140 = (bf16[1024,1024]{1,0:T(8,128)(2,1)}, bf16[1024,1024]{1,0:T(8,128)(2,1)}, bf16[2304,2176]{1,0:T(8,128)(2,1)}) custom-call(s32[4,12]{1,0:T(4,128)} %add_add_fusion.info_ref, bf16[2304,4096]{1,0:T(8,128)(2,1)} %all-gather.6.cloned.1.call-done.q_ref.k_ref.v_ref, bf16[2304,4096]{1,0:T(8,128)(2,1)} %all-gather.6.cloned.1.call-done.q_ref.k_ref.v_ref, ...), custom_call_target="tpu_custom_call" | custom-call | flops 6442450944 | bytes 28311552 | tf_op jit(solution)/shard_map/pallas_call | solution.py:163
  341.8 4.7 select_bitcast_fusion
  346.5 0.3 collective-permute-start.2
  346.8 8.5 %collective-permute-done.2 = bf16[8,144,2176]{2,1,0:T(8,128)(2,1)} collective-permute-done((bf16[8,144,2176]{2,1,0:T(8,128)(2,1)S(1)}, bf16[8,144,2176]{2,1,0:T(8,128)(2,1)}, u32[]{:S(2)}, u32[]{:S(2)}) %collective-permute-start.2) | collective-permute-done | bytes 5013536 | tf_op jit(solution)/shard_map/ppermute | solution.py:289
  355.3 9.8 %fusion = bf16[8,144,2176]{2,1,0:T(8,128)(2,1)} fusion(bf16[8,144,2176]{2,1,0:T(8,128)(2,1)} %collective-permute-done.2, pred[]{:T(512)S(6)} %eq.28, bf16[8,2,144,2176]{3,2,1,0:T(8,128)(2,1)} %bitcast.34), kind=kLoop, calls=%fused_computation.1 | loop fusion | flops 12533760 | bytes 20054016 | tf_op jit(solution)/shard_map/convert_element_type | solution.py:290
  365.1 52.5 %all-gather.8.cloned.1.call-done.w_ref = bf16[4608,2048]{1,0:T(8,128)(2,1)} async-done(((bf16[288,2048]{1,0:T(8,128)(2,1)}), bf16[4608,2048]{1,0:T(8,128)(2,1)}) %all-gather.8.cloned.1.call-update) | async-done | bytes 18874384 | tf_op jit(solution)/shard_map/all_gather | solution.py:279
  417.6 0.0 reduce-scatter.2.cloned.1.call-update
  417.7 103.3 %reduce-scatter.2.cloned.1.call-done = bf16[144,2176]{1,0:T(8,128)(2,1)} async-done(((bf16[1152,2176]{1,0:T(8,128)(2,1)}), bf16[144,2176]{1,0:T(8,128)(2,1)}) %reduce-scatter.2.cloned.1.call-update) | async-done | bytes 626704 | tf_op jit(solution)/shard_map/reduce_scatter | solution.py:292
  521.0 0.8 slice.21
  521.8 1.2 convert_element_type.62
  523.0 0.4 div.42
  523.3 1.3 fusion.5.x_ref
  524.6 7.8 %shard_map.142 = bf16[144,2304]{1,0:T(8,128)(2,1)} custom-call(s32[1]{0:T(128)} %bitcast.9.half_ref, bf16[144,2048]{1,0:T(8,128)(2,1)} %fusion.5.x_ref, bf16[4608,2048]{1,0:T(8,128)(2,1)} %all-gather.8.cloned.1.call-done.w_ref), custom_call_target="tpu_custom_call" | custom-call | flops 1358954496 | bytes 9437184 | tf_op jit(solution)/shard_map/pallas_call | solution.py:205
  532.5 1.5 collective-permute-start.3
  533.9 0.0 copy-start.2
  533.9 7.9 %shard_map.141 = bf16[144,2304]{1,0:T(8,128)(2,1)} custom-call(s32[1]{0:T(128)} %bitcast.half_ref, bf16[144,2048]{1,0:T(8,128)(2,1)} %fusion.5.x_ref, bf16[4608,2048]{1,0:T(8,128)(2,1)} %all-gather.8.cloned.1.call-done.w_ref), custom_call_target="tpu_custom_call" | custom-call | flops 1358954496 | bytes 9437184 | tf_op jit(solution)/shard_map/pallas_call | solution.py:205
  541.8 6.7 %collective-permute-done.3 = bf16[144,2304]{1,0:T(8,128)(2,1)S(1)} collective-permute-done((bf16[144,2304]{1,0:T(8,128)(2,1)}, bf16[144,2304]{1,0:T(8,128)(2,1)S(1)}, u32[]{:S(2)}, u32[]{:S(2)}) %collective-permute-start.3) | collective-permute-done | bytes 663584 | tf_op jit(solution)/shard_map/ppermute | solution.py:306
  548.5 1.4 multiply_reduce_fusion
  549.9 1.5 collective-permute-start.4
  551.4 0.0 copy-done.2
  551.4 2.1 collective-permute-done.4
  553.5 2.3 add_convert_fusion
  (8 shorter events, 0.1 us)
Async XLA Ops:
  7.2 194.0 %all-gather.4.cloned.1.call-start = ((), (), s32[]{:S(2)}) async-start(), calls=%async_computation.1 | async-start | bytes 40108032 | tf_op jit(solution)/shard_map/all_gather | solution.py:242
  10.5 0.7 copy-start.1
  10.5 3.7 copy-start
  10.5 4.1 copy-start.3
  10.5 4.1 copy-start.4
  10.5 306.5 %all-gather.6.cloned.1.call-start = ((), (), s32[]{:S(2)}) async-start(), calls=%async_computation.2 | async-start | bytes 20054016 | tf_op jit(solution)/shard_map/all_gather | solution.py:277
  11.2 4.6 collective-permute-start.1
  14.1 16.4 %collective-permute-start = (bf16[144,2304]{1,0:T(8,128)(2,1)S(1)}, bf16[144,2304]{1,0:T(8,128)(2,1)S(1)}, u32[]{:S(2)}, u32[]{:S(2)}) collective-permute-start(bf16[144,2304]{1,0:T(8,128)(2,1)S(1)} %copy-done), channel_id=1, source_target_pairs={{0,1},{1,0},{2,3},{3,2},{4,5},{5,4},{6,7},{7,6},{8,9},{9,8},{10,11... | collective-permute-start | bytes 1990664 | tf_op jit(solution)/shard_map/ppermute | solution.py:245
  217.9 99.3 %copy-start.5 = (s32[12]{0:T(128)S(1)}, s32[12]{0:T(128)}, u32[]{:S(2)}) copy-start(s32[12]{0:T(128)} %param.23) | copy-start | bytes 148
  217.9 199.7 %all-gather.8.cloned.1.call-start = ((), (), s32[]{:S(2)}) async-start(), calls=%async_computation.3 | async-start | bytes 20054016 | tf_op jit(solution)/shard_map/all_gather | solution.py:279
  317.0 204.0 %reduce-scatter.2.cloned.1.call-start = ((), (), s32[]{:S(2)}) async-start(), calls=%async_computation.4 | async-start | bytes 5640192 | tf_op jit(solution)/shard_map/reduce_scatter | solution.py:292
  346.5 8.8 %collective-permute-start.2 = (bf16[8,144,2176]{2,1,0:T(8,128)(2,1)S(1)}, bf16[8,144,2176]{2,1,0:T(8,128)(2,1)}, u32[]{:S(2)}, u32[]{:S(2)}) collective-permute-start(bf16[8,144,2176]{2,1,0:T(8,128)(2,1)S(1)} %select_bitcast_fusion), channel_id=1, source_target_pairs={{0,2},{2,0},{4,6},{6,4},{8,10},{10,8},{12,14},{14,12},{16,18},{18,... | collective-permute-start | bytes 15040520 | tf_op jit(solution)/shard_map/ppermute | solution.py:289
  532.5 16.0 %collective-permute-start.3 = (bf16[144,2304]{1,0:T(8,128)(2,1)}, bf16[144,2304]{1,0:T(8,128)(2,1)S(1)}, u32[]{:S(2)}, u32[]{:S(2)}) collective-permute-start(bf16[144,2304]{1,0:T(8,128)(2,1)} %shard_map.142), channel_id=1, source_target_pairs={{0,1},{1,0},{2,3},{3,2},{4,5},{5,4},{6,7},{7,6},{8,9},{9,8},{10,11... | collective-permute-start | bytes 1990664 | tf_op jit(solution)/shard_map/ppermute | solution.py:306
  533.9 17.5 %copy-start.2 = (bf16[2304]{0:T(1024)(128)(2,1)S(1)}, bf16[2304]{0:T(1024)(128)(2,1)}, u32[]{:S(2)}) copy-start(bf16[2304]{0:T(1024)(128)(2,1)} %param.18) | copy-start | bytes 13828
  549.9 3.6 collective-permute-start.4
Sparse Core Ops, SparseCore 0:
  10.6 190.5 all-gather.3
  218.0 98.9 all-gather.5
  318.6 98.9 all-gather.7
  421.1 99.8 reduce-scatter.1

commit v3 on v2

--- a/solution.py
+++ b/solution.py
@@ -219,6 +219,29 @@
             flops=2 * rows * depth * cols, bytes_accessed=2 * depth * cols, transcendentals=0
         ),
     )(half.reshape(1).astype(jnp.int32), attended, w_out)
+
+
+def pair_sum(blocks, stride, count):
+    side = lax.axis_index("gx") // stride % 2
+    given = lax.dynamic_index_in_dim(blocks, 1 - side, 1, keepdims=False)
+    taken = lax.ppermute(given, "gx", [(i, i ^ stride) for i in range(count)])
+    kept = lax.dynamic_index_in_dim(blocks, side, 1, keepdims=False)
+    return (kept.astype(jnp.float32) + taken.astype(jnp.float32)).astype(jnp.bfloat16)
+
+
+def scatter_sum(part, tok_rows):
+    cols = part.shape[1]
+    count = part.shape[0] // tok_rows
+    outer = count // 4
+    chip = pair_sum(part.reshape(count // 2, 2, tok_rows, cols), 1, count)
+    blocks = pair_sum(chip.reshape(outer, 2, tok_rows, cols), 2, count)
+    place = lax.axis_index("gx") // 4
+    total = lax.dynamic_index_in_dim(blocks, place, 0, keepdims=False).astype(jnp.float32)
+    for shift in range(1, outer):
+        given = lax.dynamic_index_in_dim(blocks, (place + shift) % outer, 0, keepdims=False)
+        peers = [(i, (i // 4 + shift) % outer * 4 + i % 4) for i in range(count)]
+        total = total + lax.ppermute(given, "gx", peers).astype(jnp.float32)
+    return total
 
 
 def on_device(
@@ -281,21 +304,14 @@
     first = jnp.full((REQS,), lax.axis_index("gx") * slab, jnp.int32)
     info = jnp.stack([cached_len, new_len, slot_offset, first])
     k_pool, v_pool, num_den = attend(info, qkv, k_cache, v_cache)
-    n_gx = num_den.shape[0] // tok_rows
-    core = lax.axis_index("gx") % 2
-    halves = num_den.reshape(n_gx // 2, 2, tok_rows, num_den.shape[1])
-    kept = jnp.where(core == 0, halves[:, 0], halves[:, 1])
-    given = jnp.where(core == 0, halves[:, 1], halves[:, 0])
-    taken = lax.ppermute(given, "gx", [(i, i ^ 1) for i in range(n_gx)])
-    chip = (kept.astype(jnp.float32) + taken.astype(jnp.float32)).astype(jnp.bfloat16)
-    chip, w_out = lax.optimization_barrier((chip, w_out))
-    sums = lax.psum_scatter(
-        chip.reshape(n_gx // 2 * tok_rows, num_den.shape[1]),
-        "gx",
-        scatter_dimension=0,
-        axis_index_groups=[list(range(c, n_gx, 2)) for c in range(2)],
-        tiled=True,
-    ).astype(jnp.float32)
+    half_cols = (q_cols // HD + 1) // 2 * HD
+    sums = jnp.concatenate(
+        [
+            scatter_sum(num_den[:, :half_cols], tok_rows),
+            scatter_sum(num_den[:, half_cols:], tok_rows),
+        ],
+        axis=1,
+    )
     heads = q_cols // HD
     head_num = sums[:, :q_cols].reshape(tok_rows, heads, HD)
     head_den = sums[:, q_cols : q_cols + heads]

time: 563 us -> 544 us (0.966)
  waiting for transfers between devices: 456 us -> 410 us
  local copies, waits for them, and re-layouts: 1.84 us -> 17.2 us
  starting transfers between devices: 6.9 us -> 15.5 us
    ppermute x1 -> x10, waiting for transfers between devices: 8.47 us -> 119 us  [the longest x4 96.8 us: pair_sum(): taken = lax.ppermute(given, 'gx', [(i, i ^ stride) for i in range(count)])]
    reduce_scatter x1 -> x0, waiting for transfers between devices: 103 us -> none  [on_device(): lax.psum_scatter(chip.reshape(n_gx // 2 * tok_rows, num_den.shape[1]), 'g...]
    all_gather x1, waiting for transfers between devices: 52.5 us -> 0.01 us  [on_device(): w_out = lax.all_gather(w_o_t, 'gx', axis=0, tiled=True)]
    ppermute x1 -> x10, starting transfers between devices: 0.34 us -> 9.02 us  [the longest x6 7.02 us: scatter_sum(): total = total + lax.ppermute(given, 'gx', peers).astype(jnp.float32)]
    slice x0 -> x2, local copies, waits for them, and re-layouts: none -> 7.89 us  [the longest x1 4.92 us: on_device(): num_den[:, :half_cols]]
    squeeze x0 -> x6, local copies, waits for them, and re-layouts: none -> 5.66 us  [the longest x4 4.6 us: pair_sum(): given = lax.dynamic_index_in_dim(blocks, 1 - side, 1, keepdims=False)]
  transfers between devices with their start and end apart: 9 -> 17, of which waited for: 8 -> 10; matrix products, arithmetic and copies ran while one was open for 3% -> 6% of each run, Pallas kernels for 6% -> 6%
where the time goes in v3:
time: 544 us; the launch traced here: 540 us
  waiting for transfers between devices  410 us (75%)
  Pallas kernels  58.8 us (11%)
  other arithmetic  24.9 us (5%)
  local copies, waits for them, and re-layouts  17.2 us (3%)
  starting transfers between devices  15.5 us (3%)
  between operations  13.9 us (3%)
    all_gather x1, waiting for transfers between devices, on_device(): lax.all_gather(jnp.concatenate([w_q, w_k, w_v], axis=1), 'gx', axis=0, ti...  169 us
    all_gather x1, waiting for transfers between devices, on_device(): qkv = lax.all_gather(qkv_new, 'gx', axis=0, tiled=True)  99.1 us
    ppermute x4, waiting for transfers between devices, pair_sum(): taken = lax.ppermute(given, 'gx', [(i, i ^ stride) for i in range(count)])  96.8 us
    pallas_call x1, Pallas kernels, attend(): pl.pallas_call(functools.partial(attend_kernel, group, slab), grid=(kv,),...  26.4 us
    ppermute x6, waiting for transfers between devices, scatter_sum(): total = total + lax.ppermute(given, 'gx', peers).astype(jnp.float32)  22.2 us
    pallas_call x1, Pallas kernels, project(): pl.pallas_call(functools.partial(project_kernel, q_cols // width, rope_co...  16.7 us
    pallas_call x2, Pallas kernels, out_half(): pl.pallas_call(out_kernel, grid_spec=pltpu.PrefetchScalarGridSpec(num_sca...  15.7 us
    ppermute x1, waiting for transfers between devices, on_device(): other_in = lax.ppermute(tokens, 'gy', swap)  14.7 us
  transfers between devices with their start and end apart: 17, of which 10 were waited for; matrix products, arithmetic and copies ran while one was open for 6% of the time, Pallas kernels for 6%

profile of v3, /device:TPU:0, one launch (start us, length us, event | category | flops | bytes accessed | tf_op | source)
XLA Modules:
  0.0 540.4 jit_solution(9665413613798374605)
XLA Ops:
  7.2 0.0 all-gather.4.cloned.1.call-start
  7.2 3.3 pad_maximum_fusion
  10.5 0.0 all-gather.4.cloned.1.call-update
  10.5 0.0 all-gather.6.cloned.1.call-start
  10.6 0.6 copy-done.8
  11.2 3.0 collective-permute-start.1
  14.1 0.4 collective-permute-start
  14.6 0.1 select_reduce_fusion.1
  14.7 0.3 fusion.13
  15.1 0.8 pad_maximum_fusion.2
  15.8 0.0 collective-permute-done.1
  15.8 14.7 %collective-permute-done = bf16[144,2304]{1,0:T(8,128)(2,1)S(1)} collective-permute-done((bf16[144,2304]{1,0:T(8,128)(2,1)S(1)}, bf16[144,2304]{1,0:T(8,128)(2,1)S(1)}, u32[]{:S(2)}, u32[]{:S(2)}) %collective-permute-start) | collective-permute-done | bytes 663584 | tf_op jit(solution)/shard_map/ppermute | solution.py:268
  30.5 0.5 fusion.2
  31.0 1.6 fusion.4.x_ref
  32.6 168.6 %all-gather.4.cloned.1.call-done.w_ref = bf16[4608,4096]{1,0:T(8,128)(2,1)} async-done(((bf16[288,4096]{1,0:T(8,128)(2,1)}), bf16[4608,4096]{1,0:T(8,128)(2,1)}) %all-gather.4.cloned.1.call-update) | async-done | bytes 37748752 | tf_op jit(solution)/shard_map/all_gather | solution.py:265
  201.2 16.7 %shard_map.139 = bf16[144,4096]{1,0:T(8,128)(2,1)} custom-call(bf16[144,4608]{1,0:T(8,128)(2,1)} %fusion.4.x_ref, bf16[4608,4096]{1,0:T(8,128)(2,1)} %all-gather.4.cloned.1.call-done.w_ref, f32[144,128]{1,0:T(8,128)} %get-tuple-element.24.cos_ref, f32[144,128]{1,0:T(8,128)} %get-tuple-element.25.sin_ref), custom_call_target="tpu_custom_call" | custom-call | flops 5435817984 | bytes 37748736 | tf_op jit(solution)/shard_map/pallas_call | solution.py:48
  217.9 0.0 all-gather.6.cloned.1.call-update
  217.9 0.0 all-gather.8.cloned.1.call-start
  218.0 99.1 %all-gather.6.cloned.1.call-done.q_ref.k_ref.v_ref = bf16[2304,4096]{1,0:T(8,128)(2,1)} async-done(((bf16[144,4096]{1,0:T(8,128)(2,1)}), bf16[2304,4096]{1,0:T(8,128)(2,1)}) %all-gather.6.cloned.1.call-update) | async-done | bytes 18874384 | tf_op jit(solution)/shard_map/all_gather | solution.py:300
  317.0 0.0 all-gather.8.cloned.1.call-update
  317.1 0.1 pad.20.clone
  317.1 0.6 add_add_fusion.info_ref
  317.8 26.4 %shard_map.140 = (bf16[1024,1024]{1,0:T(8,128)(2,1)}, bf16[1024,1024]{1,0:T(8,128)(2,1)}, bf16[2304,2176]{1,0:T(8,128)(2,1)}) custom-call(s32[4,12]{1,0:T(4,128)} %add_add_fusion.info_ref, bf16[2304,4096]{1,0:T(8,128)(2,1)} %all-gather.6.cloned.1.call-done.q_ref.k_ref.v_ref, bf16[2304,4096]{1,0:T(8,128)(2,1)} %all-gather.6.cloned.1.call-done.q_ref.k_ref.v_ref, ...), custom_call_target="tpu_custom_call" | custom-call | flops 6442450944 | bytes 28311552 | tf_op jit(solution)/shard_map/pallas_call | solution.py:163
  344.2 3.0 slice.13
  347.2 4.9 slice.12
  352.2 2.0 dynamic-slice_bitcast_fusion.1
  354.2 0.8 copy-done.2
  355.0 0.0 collective-permute-start.2
  355.0 0.2 dynamic-slice_bitcast_fusion
  355.2 0.6 collective-permute-start.7
  355.8 4.6 collective-permute-done.2
  360.4 3.8 fusion.1
  364.2 1.2 dynamic-slice_bitcast_fusion.3
  365.4 0.6 copy-done.3
  366.0 2.5 fusion
  368.5 1.2 dynamic-slice_bitcast_fusion.2
  369.7 1.4 collective-permute-start.8
  371.2 48.6 %collective-permute-done.3 = bf16[4,144,1024]{2,1,0:T(8,128)(2,1)} collective-permute-done((bf16[4,144,1024]{2,1,0:T(8,128)(2,1)}, bf16[4,144,1024]{2,1,0:T(8,128)(2,1)}, u32[]{:S(2)}, u32[]{:S(2)}) %collective-permute-start.3) | collective-permute-done | bytes 1179680 | tf_op jit(solution)/shard_map/ppermute | solution.py:227
  419.8 2.1 fusion.6
  421.9 1.0 dynamic-slice_bitcast_fusion.9
  422.9 2.4 collective-permute-start.6
  425.4 0.6 collective-permute-start.4
  425.9 43.6 %collective-permute-done.8 = bf16[4,144,1152]{2,1,0:T(8,128)(2,1)} collective-permute-done((bf16[4,144,1152]{2,1,0:T(8,128)(2,1)}, bf16[4,144,1152]{2,1,0:T(8,128)(2,1)}, u32[]{:S(2)}, u32[]{:S(2)}) %collective-permute-start.8) | collective-permute-done | bytes 1327136 | tf_op jit(solution)/shard_map/ppermute | solution.py:227
  469.5 1.6 fusion.5
  471.1 1.1 copy-done.5
  472.2 0.1 dynamic-slice_bitcast_fusion.6
  472.3 3.4 collective-permute-start.11
  475.7 0.0 collective-permute-start.10
  475.7 0.6 collective-permute-start.9
  476.3 0.1 copy-done.7
  476.4 1.4 fusion.12
  477.9 8.8 %collective-permute-done.11 = bf16[144,1152]{1,0:T(8,128)(2,1)S(1)} collective-permute-done((bf16[144,1152]{1,0:T(8,128)(2,1)S(1)}, bf16[144,1152]{1,0:T(8,128)(2,1)S(1)}, u32[]{:S(2)}, u32[]{:S(2)}) %collective-permute-start.11) | collective-permute-done | bytes 331808 | tf_op jit(solution)/shard_map/ppermute | solution.py:243
  486.7 13.4 %collective-permute-done.10 = bf16[144,1152]{1,0:T(8,128)(2,1)S(1)} collective-permute-done((bf16[144,1152]{1,0:T(8,128)(2,1)S(1)}, bf16[144,1152]{1,0:T(8,128)(2,1)S(1)}, u32[]{:S(2)}, u32[]{:S(2)}) %collective-permute-start.10) | collective-permute-done | bytes 331808 | tf_op jit(solution)/shard_map/ppermute | solution.py:243
  500.1 1.2 fusion.10
  501.3 0.4 div.67
  501.6 1.4 fusion.8.x_ref
  503.0 7.8 %shard_map.142 = bf16[144,2304]{1,0:T(8,128)(2,1)} custom-call(s32[1]{0:T(128)} %bitcast.25.half_ref, bf16[144,2048]{1,0:T(8,128)(2,1)} %fusion.8.x_ref, bf16[4608,2048]{1,0:T(8,128)(2,1)} %all-gather.8.cloned.1.call-done.w_ref), custom_call_target="tpu_custom_call" | custom-call | flops 1358954496 | bytes 9437184 | tf_op jit(solution)/shard_map/pallas_call | solution.py:205
  510.8 1.5 collective-permute-start.12
  512.3 7.9 %shard_map.141 = bf16[144,2304]{1,0:T(8,128)(2,1)} custom-call(s32[1]{0:T(128)} %bitcast.half_ref, bf16[144,2048]{1,0:T(8,128)(2,1)} %fusion.8.x_ref, bf16[4608,2048]{1,0:T(8,128)(2,1)} %all-gather.8.cloned.1.call-done.w_ref), custom_call_target="tpu_custom_call" | custom-call | flops 1358954496 | bytes 9437184 | tf_op jit(solution)/shard_map/pallas_call | solution.py:205
  520.2 6.4 %collective-permute-done.12 = bf16[144,2304]{1,0:T(8,128)(2,1)S(1)} collective-permute-done((bf16[144,2304]{1,0:T(8,128)(2,1)}, bf16[144,2304]{1,0:T(8,128)(2,1)S(1)}, u32[]{:S(2)}, u32[]{:S(2)}) %collective-permute-start.12) | collective-permute-done | bytes 663584 | tf_op jit(solution)/shard_map/ppermute | solution.py:322
  526.5 1.4 multiply_reduce_fusion
  527.9 1.5 collective-permute-start.13
  529.5 2.1 collective-permute-done.13
  531.5 2.3 add_convert_fusion
  (38 shorter events, 0.2 us)
Async XLA Ops:
  7.2 194.0 %all-gather.4.cloned.1.call-start = ((), (), s32[]{:S(2)}) async-start(), calls=%async_computation | async-start | bytes 40108032 | tf_op jit(solution)/shard_map/all_gather | solution.py:265
  10.5 0.7 copy-start.8
  10.5 3.7 copy-start.4
  10.5 4.1 copy-start.10
  10.5 4.1 copy-start.11
  10.5 306.5 %all-gather.6.cloned.1.call-start = ((), (), s32[]{:S(2)}) async-start(), calls=%async_computation.1 | async-start | bytes 20054016 | tf_op jit(solution)/shard_map/all_gather | solution.py:300
  11.2 4.7 collective-permute-start.1
  14.1 16.4 %collective-permute-start = (bf16[144,2304]{1,0:T(8,128)(2,1)S(1)}, bf16[144,2304]{1,0:T(8,128)(2,1)S(1)}, u32[]{:S(2)}, u32[]{:S(2)}) collective-permute-start(bf16[144,2304]{1,0:T(8,128)(2,1)S(1)} %copy-done.4), channel_id=1, source_target_pairs={{0,1},{1,0},{2,3},{3,2},{4,5},{5,4},{6,7},{7,6},{8,9},{9,8},{10,11... | collective-permute-start | bytes 1990664 | tf_op jit(solution)/shard_map/ppermute | solution.py:268
  217.9 99.3 %copy-start.12 = (s32[12]{0:T(128)S(1)}, s32[12]{0:T(128)}, u32[]{:S(2)}) copy-start(s32[12]{0:T(128)} %param.23) | copy-start | bytes 148
  217.9 285.1 %all-gather.8.cloned.1.call-start = ((), (), s32[]{:S(2)}) async-start(), calls=%async_computation.2 | async-start | bytes 20054016 | tf_op jit(solution)/shard_map/all_gather | solution.py:302
  347.2 7.8 %copy-start = (bf16[2304,1152]{1,0:T(8,128)(2,1)}, bf16[2304,1152]{1,0:T(8,128)(2,1)S(1)}, u32[]{:S(2)}) copy-start(bf16[2304,1152]{1,0:T(8,128)(2,1)S(1)} %slice.13) | copy-start | bytes 15925252
  352.1 2.8 copy-start.2
  355.0 5.4 %collective-permute-start.2 = (bf16[8,144,1024]{2,1,0:T(8,128)(2,1)}, bf16[8,144,1024]{2,1,0:T(8,128)(2,1)}, u32[]{:S(2)}, u32[]{:S(2)}) collective-permute-start(bf16[8,144,1024]{2,1,0:T(8,128)(2,1)} %dynamic-slice_bitcast_fusion.1), channel_id=1, source_target_pairs={{0,2},{2,0},{4,6},{6,4},{8,10},{10,8},{12,14},{14,12},{16,18},{18,... | collective-permute-start | bytes 7077896 | tf_op jit(solution)/shard_map/ppermute | solution.py:227
  355.2 10.8 %collective-permute-start.7 = (bf16[8,144,1152]{2,1,0:T(8,128)(2,1)S(1)}, bf16[8,144,1152]{2,1,0:T(8,128)(2,1)}, u32[]{:S(2)}, u32[]{:S(2)}) collective-permute-start(bf16[8,144,1152]{2,1,0:T(8,128)(2,1)S(1)} %dynamic-slice_bitcast_fusion), channel_id=1, source_target_pairs={{0,2},{2,0},{4,6},{6,4},{8,10},{10,8},{12,14},{14,12},{16,18},{18,... | collective-permute-start | bytes 7962632 | tf_op jit(solution)/shard_map/ppermute | solution.py:227
  360.4 5.6 %copy-start.1 = (bf16[2304,1152]{1,0:T(8,128)(2,1)S(1)}, bf16[2304,1152]{1,0:T(8,128)(2,1)}, u32[]{:S(2)}) copy-start(bf16[2304,1152]{1,0:T(8,128)(2,1)} %copy-done) | copy-start | bytes 15925252
  364.2 1.8 copy-start.3
  365.4 54.4 %collective-permute-start.3 = (bf16[4,144,1024]{2,1,0:T(8,128)(2,1)}, bf16[4,144,1024]{2,1,0:T(8,128)(2,1)}, u32[]{:S(2)}, u32[]{:S(2)}) collective-permute-start(bf16[4,144,1024]{2,1,0:T(8,128)(2,1)} %dynamic-slice_bitcast_fusion.3), channel_id=1, source_target_pairs={{0,4},{2,6},{4,0},{6,2},{8,12},{10,14},{12,8},{14,10},{16,20},{18,... | collective-permute-start | bytes 3538952 | tf_op jit(solution)/shard_map/ppermute | solution.py:227
  369.7 99.7 %collective-permute-start.8 = (bf16[4,144,1152]{2,1,0:T(8,128)(2,1)}, bf16[4,144,1152]{2,1,0:T(8,128)(2,1)}, u32[]{:S(2)}, u32[]{:S(2)}) collective-permute-start(bf16[4,144,1152]{2,1,0:T(8,128)(2,1)} %dynamic-slice_bitcast_fusion.2), channel_id=1, source_target_pairs={{0,4},{2,6},{4,0},{6,2},{8,12},{10,14},{12,8},{14,10},{16,20},{18,... | collective-permute-start | bytes 3981320 | tf_op jit(solution)/shard_map/ppermute | solution.py:227
  421.9 4.0 copy-start.6
  422.9 52.8 %collective-permute-start.6 = (bf16[144,1024]{1,0:T(8,128)(2,1)S(1)}, bf16[144,1024]{1,0:T(8,128)(2,1)S(1)}, u32[]{:S(2)}, u32[]{:S(2)}) collective-permute-start(bf16[144,1024]{1,0:T(8,128)(2,1)S(1)} %get-tuple-element.19), channel_id=1, source_target_pairs={{0,24},{2,26},{4,28},{6,30},{8,0},{10,2},{12,4},{14,6},{16,8},{18,... | collective-permute-start | bytes 884744 | tf_op jit(solution)/shard_map/ppermute | solution.py:243
  425.3 51.1 %collective-permute-start.5 = (bf16[144,1024]{1,0:T(8,128)(2,1)}, bf16[144,1024]{1,0:T(8,128)(2,1)}, u32[]{:S(2)}, u32[]{:S(2)}) collective-permute-start(bf16[144,1024]{1,0:T(8,128)(2,1)} %get-tuple-element.20), channel_id=1, source_target_pairs={{0,16},{2,18},{4,20},{6,22},{8,24},{10,26},{12,28},{14,30},{16,0},... | collective-permute-start | bytes 884744 | tf_op jit(solution)/shard_map/ppermute | solution.py:243
  425.4 51.1 %collective-permute-start.4 = (bf16[144,1024]{1,0:T(8,128)(2,1)}, bf16[144,1024]{1,0:T(8,128)(2,1)}, u32[]{:S(2)}, u32[]{:S(2)}) collective-permute-start(bf16[144,1024]{1,0:T(8,128)(2,1)} %get-tuple-element.18), channel_id=1, source_target_pairs={{0,8},{2,10},{4,12},{6,14},{8,16},{10,18},{12,20},{14,22},{16,24},... | collective-permute-start | bytes 884744 | tf_op jit(solution)/shard_map/ppermute | solution.py:243
  471.1 1.1 copy-start.5
  472.3 14.4 %collective-permute-start.11 = (bf16[144,1152]{1,0:T(8,128)(2,1)S(1)}, bf16[144,1152]{1,0:T(8,128)(2,1)S(1)}, u32[]{:S(2)}, u32[]{:S(2)}) collective-permute-start(bf16[144,1152]{1,0:T(8,128)(2,1)S(1)} %get-tuple-element.16), channel_id=1, source_target_pairs={{0,24},{2,26},{4,28},{6,30},{8,0},{10,2},{12,4},{14,6},{16,8},{18,... | collective-permute-start | bytes 995336 | tf_op jit(solution)/shard_map/ppermute | solution.py:243
  475.7 24.4 %collective-permute-start.10 = (bf16[144,1152]{1,0:T(8,128)(2,1)S(1)}, bf16[144,1152]{1,0:T(8,128)(2,1)S(1)}, u32[]{:S(2)}, u32[]{:S(2)}) collective-permute-start(bf16[144,1152]{1,0:T(8,128)(2,1)S(1)} %get-tuple-element.17), channel_id=1, source_target_pairs={{0,16},{2,18},{4,20},{6,22},{8,24},{10,26},{12,28},{14,30},{16,0},... | collective-permute-start | bytes 995336 | tf_op jit(solution)/shard_map/ppermute | solution.py:243
  475.7 0.7 copy-start.7
  475.7 24.4 %collective-permute-start.9 = (bf16[144,1152]{1,0:T(8,128)(2,1)S(1)}, bf16[144,1152]{1,0:T(8,128)(2,1)S(1)}, u32[]{:S(2)}, u32[]{:S(2)}) collective-permute-start(bf16[144,1152]{1,0:T(8,128)(2,1)S(1)} %get-tuple-element.15), channel_id=1, source_target_pairs={{0,8},{2,10},{4,12},{6,14},{8,16},{10,18},{12,20},{14,22},{16,24},... | collective-permute-start | bytes 995336 | tf_op jit(solution)/shard_map/ppermute | solution.py:243
  510.8 15.7 %collective-permute-start.12 = (bf16[144,2304]{1,0:T(8,128)(2,1)}, bf16[144,2304]{1,0:T(8,128)(2,1)S(1)}, u32[]{:S(2)}, u32[]{:S(2)}) collective-permute-start(bf16[144,2304]{1,0:T(8,128)(2,1)} %shard_map.142), channel_id=1, source_target_pairs={{0,1},{1,0},{2,3},{3,2},{4,5},{5,4},{6,7},{7,6},{8,9},{9,8},{10,11... | collective-permute-start | bytes 1990664 | tf_op jit(solution)/shard_map/ppermute | solution.py:322
  512.3 17.1 %copy-start.9 = (bf16[2304]{0:T(1024)(128)(2,1)S(1)}, bf16[2304]{0:T(1024)(128)(2,1)}, u32[]{:S(2)}) copy-start(bf16[2304]{0:T(1024)(128)(2,1)} %param.18) | copy-start | bytes 13828
  527.9 3.6 collective-permute-start.13
Sparse Core Ops, SparseCore 0:
  10.6 190.5 all-gather.3
  218.0 98.9 all-gather.5
  318.6 146.0 all-gather.7

commit v4 on v3

--- a/solution.py
+++ b/solution.py
@@ -221,20 +221,24 @@
     )(half.reshape(1).astype(jnp.int32), attended, w_out)
 
 
-def pair_sum(blocks, stride, count):
+def pick_side(blocks, side, start, cols):
+    size = (blocks.shape[0], 1, blocks.shape[2], cols)
+    return lax.dynamic_slice(blocks, (0, side, 0, start), size)[:, 0]
+
+
+def pair_sum(blocks, stride, count, start, cols):
     side = lax.axis_index("gx") // stride % 2
-    given = lax.dynamic_index_in_dim(blocks, 1 - side, 1, keepdims=False)
+    given = pick_side(blocks, 1 - side, start, cols)
     taken = lax.ppermute(given, "gx", [(i, i ^ stride) for i in range(count)])
-    kept = lax.dynamic_index_in_dim(blocks, side, 1, keepdims=False)
+    kept = pick_side(blocks, side, start, cols)
     return (kept.astype(jnp.float32) + taken.astype(jnp.float32)).astype(jnp.bfloat16)
 
 
-def scatter_sum(part, tok_rows):
-    cols = part.shape[1]
+def scatter_sum(part, tok_rows, start, cols):
     count = part.shape[0] // tok_rows
     outer = count // 4
-    chip = pair_sum(part.reshape(count // 2, 2, tok_rows, cols), 1, count)
-    blocks = pair_sum(chip.reshape(outer, 2, tok_rows, cols), 2, count)
+    chip = pair_sum(part.reshape(count // 2, 2, tok_rows, part.shape[1]), 1, count, start, cols)
+    blocks = pair_sum(chip.reshape(outer, 2, tok_rows, cols), 2, count, 0, cols)
     place = lax.axis_index("gx") // 4
     total = lax.dynamic_index_in_dim(blocks, place, 0, keepdims=False).astype(jnp.float32)
     for shift in range(1, outer):
@@ -307,8 +311,8 @@
     half_cols = (q_cols // HD + 1) // 2 * HD
     sums = jnp.concatenate(
         [
-            scatter_sum(num_den[:, :half_cols], tok_rows),
-            scatter_sum(num_den[:, half_cols:], tok_rows),
+            scatter_sum(num_den, tok_rows, 0, half_cols),
+            scatter_sum(num_den, tok_rows, half_cols, q_cols + HD - half_cols),
         ],
         axis=1,
     )

time: 544 us -> 544 us (level)
  Pallas kernels: 58.8 us -> 66.7 us
  local copies, waits for them, and re-layouts: 17.2 us -> 11.6 us
    slice x2 -> x0, local copies, waits for them, and re-layouts: 7.89 us -> none  [the longest x1 4.92 us: on_device(): num_den[:, :half_cols]]
    pallas_call x1, Pallas kernels: 26.4 us -> 34.3 us  [attend(): pl.pallas_call(functools.partial(attend_kernel, group, slab), grid=(kv,),...]
  transfers between devices with their start and end apart: 17 -> 17, of which waited for: 10 -> 10; matrix products, arithmetic and copies ran while one was open for 6% -> 5% of each run, Pallas kernels for 6% -> 8%
where the time goes in v4:
time: 544 us; the launch traced here: 541 us
  waiting for transfers between devices  408 us (75%)
  Pallas kernels  66.7 us (12%)
  other arithmetic  25.5 us (5%)
  starting transfers between devices  14.8 us (3%)
  between operations  13.9 us (3%)
  local copies, waits for them, and re-layouts  11.6 us (2%)
    all_gather x1, waiting for transfers between devices, on_device(): lax.all_gather(jnp.concatenate([w_q, w_k, w_v], axis=1), 'gx', axis=0, ti...  169 us
    all_gather x1, waiting for transfers between devices, on_device(): qkv = lax.all_gather(qkv_new, 'gx', axis=0, tiled=True)  99.1 us
    ppermute x4, waiting for transfers between devices, pair_sum(): taken = lax.ppermute(given, 'gx', [(i, i ^ stride) for i in range(count)])  94.7 us
    pallas_call x1, Pallas kernels, attend(): pl.pallas_call(functools.partial(attend_kernel, group, slab), grid=(kv,),...  34.3 us
    ppermute x6, waiting for transfers between devices, scatter_sum(): total = total + lax.ppermute(given, 'gx', peers).astype(jnp.float32)  22.4 us
    pallas_call x1, Pallas kernels, project(): pl.pallas_call(functools.partial(project_kernel, q_cols // width, rope_co...  16.7 us
    pallas_call x2, Pallas kernels, out_half(): pl.pallas_call(out_kernel, grid_spec=pltpu.PrefetchScalarGridSpec(num_sca...  15.7 us
    ppermute x1, waiting for transfers between devices, on_device(): other_in = lax.ppermute(tokens, 'gy', swap)  14.7 us
  transfers between devices with their start and end apart: 17, of which 10 were waited for; matrix products, arithmetic and copies ran while one was open for 5% of the time, Pallas kernels for 8%

profile of v4, /device:TPU:0, one launch (start us, length us, event | category | flops | bytes accessed | tf_op | source)
XLA Modules:
  0.0 540.7 jit_solution(165694545781381011)
XLA Ops:
  7.2 0.0 all-gather.4.cloned.1.call-start
  7.2 3.3 pad_maximum_fusion
  10.5 0.0 all-gather.4.cloned.1.call-update
  10.5 0.0 all-gather.6.cloned.1.call-start
  10.6 0.6 copy-done.5
  11.2 3.0 collective-permute-start.1
  14.1 0.4 collective-permute-start
  14.6 0.1 select_reduce_fusion.1
  14.7 0.3 fusion.13
  15.0 0.8 pad_maximum_fusion.2
  15.8 0.0 collective-permute-done.1
  15.8 14.7 %collective-permute-done = bf16[144,2304]{1,0:T(8,128)(2,1)S(1)} collective-permute-done((bf16[144,2304]{1,0:T(8,128)(2,1)S(1)}, bf16[144,2304]{1,0:T(8,128)(2,1)S(1)}, u32[]{:S(2)}, u32[]{:S(2)}) %collective-permute-start) | collective-permute-done | bytes 663584 | tf_op jit(solution)/shard_map/ppermute | solution.py:272
  30.5 0.5 fusion.2
  31.0 1.6 fusion.4.x_ref
  32.5 168.6 %all-gather.4.cloned.1.call-done.w_ref = bf16[4608,4096]{1,0:T(8,128)(2,1)} async-done(((bf16[288,4096]{1,0:T(8,128)(2,1)}), bf16[4608,4096]{1,0:T(8,128)(2,1)}) %all-gather.4.cloned.1.call-update) | async-done | bytes 37748752 | tf_op jit(solution)/shard_map/all_gather | solution.py:269
  201.2 16.7 %shard_map.139 = bf16[144,4096]{1,0:T(8,128)(2,1)} custom-call(bf16[144,4608]{1,0:T(8,128)(2,1)} %fusion.4.x_ref, bf16[4608,4096]{1,0:T(8,128)(2,1)} %all-gather.4.cloned.1.call-done.w_ref, f32[144,128]{1,0:T(8,128)} %get-tuple-element.24.cos_ref, f32[144,128]{1,0:T(8,128)} %get-tuple-element.25.sin_ref), custom_call_target="tpu_custom_call" | custom-call | flops 5435817984 | bytes 37748736 | tf_op jit(solution)/shard_map/pallas_call | solution.py:48
  217.9 0.0 all-gather.6.cloned.1.call-update
  217.9 0.0 all-gather.8.cloned.1.call-start
  217.9 99.1 %all-gather.6.cloned.1.call-done.q_ref.k_ref.v_ref = bf16[2304,4096]{1,0:T(8,128)(2,1)} async-done(((bf16[144,4096]{1,0:T(8,128)(2,1)}), bf16[2304,4096]{1,0:T(8,128)(2,1)}) %all-gather.6.cloned.1.call-update) | async-done | bytes 18874384 | tf_op jit(solution)/shard_map/all_gather | solution.py:304
  317.0 0.0 all-gather.8.cloned.1.call-update
  317.0 0.1 pad.20.clone
  317.1 0.6 add_add_fusion.info_ref
  317.8 34.3 %shard_map.140 = (bf16[1024,1024]{1,0:T(8,128)(2,1)}, bf16[1024,1024]{1,0:T(8,128)(2,1)}, bf16[2304,2176]{1,0:T(8,128)(2,1)}) custom-call(s32[4,12]{1,0:T(4,128)} %add_add_fusion.info_ref, bf16[2304,4096]{1,0:T(8,128)(2,1)} %all-gather.6.cloned.1.call-done.q_ref.k_ref.v_ref, bf16[2304,4096]{1,0:T(8,128)(2,1)} %all-gather.6.cloned.1.call-done.q_ref.k_ref.v_ref, ...), custom_call_target="tpu_custom_call" | custom-call | flops 6442450944 | bytes 28311552 | tf_op jit(solution)/shard_map/pallas_call | solution.py:163
  352.1 3.3 dynamic-slice_bitcast_fusion.1
  355.4 0.0 collective-permute-start.2
  355.4 2.0 dynamic-slice_bitcast_fusion
  357.4 0.7 collective-permute-start.7
  358.1 2.6 collective-permute-done.2
  360.7 3.6 fusion.1
  364.3 1.3 dynamic-slice_bitcast_fusion.3
  365.6 0.0 collective-permute-start.3
  365.6 0.5 copy-done
  366.1 0.0 collective-permute-done.7
  366.1 3.3 fusion
  369.4 1.2 dynamic-slice_bitcast_fusion.2
  370.6 1.6 collective-permute-start.8
  372.2 47.8 %collective-permute-done.3 = bf16[4,144,1024]{2,1,0:T(8,128)(2,1)} collective-permute-done((bf16[4,144,1024]{2,1,0:T(8,128)(2,1)}, bf16[4,144,1024]{2,1,0:T(8,128)(2,1)}, u32[]{:S(2)}, u32[]{:S(2)}) %collective-permute-start.3) | collective-permute-done | bytes 1179680 | tf_op jit(solution)/shard_map/ppermute | solution.py:232
  420.0 2.1 fusion.6
  422.2 1.0 dynamic-slice_bitcast_fusion.9
  423.1 0.0 collective-permute-start.6
  423.1 0.0 collective-permute-start.5
  423.1 2.0 collective-permute-start.4
  425.2 44.3 %collective-permute-done.8 = bf16[4,144,1152]{2,1,0:T(8,128)(2,1)} collective-permute-done((bf16[4,144,1152]{2,1,0:T(8,128)(2,1)}, bf16[4,144,1152]{2,1,0:T(8,128)(2,1)}, u32[]{:S(2)}, u32[]{:S(2)}) %collective-permute-start.8) | collective-permute-done | bytes 1327136 | tf_op jit(solution)/shard_map/ppermute | solution.py:232
  469.5 1.6 fusion.5
  471.1 1.1 copy-done.2
  472.2 0.1 dynamic-slice_bitcast_fusion.6
  472.3 3.4 collective-permute-start.11
  475.7 0.6 collective-permute-start.9
  476.3 0.1 copy-done.4
  476.5 1.4 fusion.12
  477.9 8.8 %collective-permute-done.11 = bf16[144,1152]{1,0:T(8,128)(2,1)S(1)} collective-permute-done((bf16[144,1152]{1,0:T(8,128)(2,1)S(1)}, bf16[144,1152]{1,0:T(8,128)(2,1)S(1)}, u32[]{:S(2)}, u32[]{:S(2)}) %collective-permute-start.11) | collective-permute-done | bytes 331808 | tf_op jit(solution)/shard_map/ppermute | solution.py:247
  486.7 13.5 %collective-permute-done.10 = bf16[144,1152]{1,0:T(8,128)(2,1)S(1)} collective-permute-done((bf16[144,1152]{1,0:T(8,128)(2,1)S(1)}, bf16[144,1152]{1,0:T(8,128)(2,1)S(1)}, u32[]{:S(2)}, u32[]{:S(2)}) %collective-permute-start.10) | collective-permute-done | bytes 331808 | tf_op jit(solution)/shard_map/ppermute | solution.py:247
  500.2 0.0 collective-permute-done.9
  500.2 1.2 fusion.10
  501.4 0.4 div.67
  501.8 1.3 fusion.8.x_ref
  503.1 7.8 %shard_map.142 = bf16[144,2304]{1,0:T(8,128)(2,1)} custom-call(s32[1]{0:T(128)} %bitcast.24.half_ref, bf16[144,2048]{1,0:T(8,128)(2,1)} %fusion.8.x_ref, bf16[4608,2048]{1,0:T(8,128)(2,1)} %all-gather.8.cloned.1.call-done.w_ref), custom_call_target="tpu_custom_call" | custom-call | flops 1358954496 | bytes 9437184 | tf_op jit(solution)/shard_map/pallas_call | solution.py:205
  511.0 1.5 collective-permute-start.12
  512.4 7.9 %shard_map.141 = bf16[144,2304]{1,0:T(8,128)(2,1)} custom-call(s32[1]{0:T(128)} %bitcast.half_ref, bf16[144,2048]{1,0:T(8,128)(2,1)} %fusion.8.x_ref, bf16[4608,2048]{1,0:T(8,128)(2,1)} %all-gather.8.cloned.1.call-done.w_ref), custom_call_target="tpu_custom_call" | custom-call | flops 1358954496 | bytes 9437184 | tf_op jit(solution)/shard_map/pallas_call | solution.py:205
  520.3 6.5 %collective-permute-done.12 = bf16[144,2304]{1,0:T(8,128)(2,1)S(1)} collective-permute-done((bf16[144,2304]{1,0:T(8,128)(2,1)}, bf16[144,2304]{1,0:T(8,128)(2,1)S(1)}, u32[]{:S(2)}, u32[]{:S(2)}) %collective-permute-start.12) | collective-permute-done | bytes 663584 | tf_op jit(solution)/shard_map/ppermute | solution.py:326
  526.8 1.4 multiply_reduce_fusion
  528.2 1.5 collective-permute-start.13
  529.7 2.1 collective-permute-done.13
  531.8 2.3 add_convert_fusion
  (30 shorter events, 0.1 us)
Async XLA Ops:
  7.2 194.0 %all-gather.4.cloned.1.call-start = ((), (), s32[]{:S(2)}) async-start(), calls=%async_computation | async-start | bytes 40108032 | tf_op jit(solution)/shard_map/all_gather | solution.py:269
  10.5 0.7 copy-start.5
  10.5 3.7 copy-start.1
  10.5 4.1 copy-start.7
  10.5 4.1 copy-start.8
  10.5 306.5 %all-gather.6.cloned.1.call-start = ((), (), s32[]{:S(2)}) async-start(), calls=%async_computation.1 | async-start | bytes 20054016 | tf_op jit(solution)/shard_map/all_gather | solution.py:304
  11.2 4.6 collective-permute-start.1
  14.1 16.4 %collective-permute-start = (bf16[144,2304]{1,0:T(8,128)(2,1)S(1)}, bf16[144,2304]{1,0:T(8,128)(2,1)S(1)}, u32[]{:S(2)}, u32[]{:S(2)}) collective-permute-start(bf16[144,2304]{1,0:T(8,128)(2,1)S(1)} %copy-done.1), channel_id=1, source_target_pairs={{0,1},{1,0},{2,3},{3,2},{4,5},{5,4},{6,7},{7,6},{8,9},{9,8},{10,11... | collective-permute-start | bytes 1990664 | tf_op jit(solution)/shard_map/ppermute | solution.py:272
  217.9 99.3 %copy-start.9 = (s32[12]{0:T(128)S(1)}, s32[12]{0:T(128)}, u32[]{:S(2)}) copy-start(s32[12]{0:T(128)} %param.23) | copy-start | bytes 148
  217.9 285.2 %all-gather.8.cloned.1.call-start = ((), (), s32[]{:S(2)}) async-start(), calls=%async_computation.2 | async-start | bytes 20054016 | tf_op jit(solution)/shard_map/all_gather | solution.py:306
  355.4 5.3 collective-permute-start.2
  357.4 8.7 %collective-permute-start.7 = (bf16[8,144,1152]{2,1,0:T(8,128)(2,1)S(1)}, bf16[8,144,1152]{2,1,0:T(8,128)(2,1)}, u32[]{:S(2)}, u32[]{:S(2)}) collective-permute-start(bf16[8,144,1152]{2,1,0:T(8,128)(2,1)S(1)} %dynamic-slice_bitcast_fusion), channel_id=1, source_target_pairs={{0,2},{2,0},{4,6},{6,4},{8,10},{10,8},{12,14},{14,12},{16,18},{18,... | collective-permute-start | bytes 7962632 | tf_op jit(solution)/shard_map/ppermute | solution.py:232
  364.3 1.8 copy-start
  365.6 54.4 %collective-permute-start.3 = (bf16[4,144,1024]{2,1,0:T(8,128)(2,1)}, bf16[4,144,1024]{2,1,0:T(8,128)(2,1)}, u32[]{:S(2)}, u32[]{:S(2)}) collective-permute-start(bf16[4,144,1024]{2,1,0:T(8,128)(2,1)} %dynamic-slice_bitcast_fusion.3), channel_id=1, source_target_pairs={{0,4},{2,6},{4,0},{6,2},{8,12},{10,14},{12,8},{14,10},{16,20},{18,... | collective-permute-start | bytes 3538952 | tf_op jit(solution)/shard_map/ppermute | solution.py:232
  370.6 98.8 %collective-permute-start.8 = (bf16[4,144,1152]{2,1,0:T(8,128)(2,1)}, bf16[4,144,1152]{2,1,0:T(8,128)(2,1)}, u32[]{:S(2)}, u32[]{:S(2)}) collective-permute-start(bf16[4,144,1152]{2,1,0:T(8,128)(2,1)} %dynamic-slice_bitcast_fusion.2), channel_id=1, source_target_pairs={{0,4},{2,6},{4,0},{6,2},{8,12},{10,14},{12,8},{14,10},{16,20},{18,... | collective-permute-start | bytes 3981320 | tf_op jit(solution)/shard_map/ppermute | solution.py:232
  422.2 3.0 copy-start.3
  423.1 52.5 %collective-permute-start.6 = (bf16[144,1024]{1,0:T(8,128)(2,1)S(1)}, bf16[144,1024]{1,0:T(8,128)(2,1)S(1)}, u32[]{:S(2)}, u32[]{:S(2)}) collective-permute-start(bf16[144,1024]{1,0:T(8,128)(2,1)S(1)} %get-tuple-element.19), channel_id=1, source_target_pairs={{0,24},{2,26},{4,28},{6,30},{8,0},{10,2},{12,4},{14,6},{16,8},{18,... | collective-permute-start | bytes 884744 | tf_op jit(solution)/shard_map/ppermute | solution.py:247
  423.1 53.3 %collective-permute-start.5 = (bf16[144,1024]{1,0:T(8,128)(2,1)}, bf16[144,1024]{1,0:T(8,128)(2,1)}, u32[]{:S(2)}, u32[]{:S(2)}) collective-permute-start(bf16[144,1024]{1,0:T(8,128)(2,1)} %get-tuple-element.20), channel_id=1, source_target_pairs={{0,16},{2,18},{4,20},{6,22},{8,24},{10,26},{12,28},{14,30},{16,0},... | collective-permute-start | bytes 884744 | tf_op jit(solution)/shard_map/ppermute | solution.py:247
  423.1 53.3 %collective-permute-start.4 = (bf16[144,1024]{1,0:T(8,128)(2,1)}, bf16[144,1024]{1,0:T(8,128)(2,1)}, u32[]{:S(2)}, u32[]{:S(2)}) collective-permute-start(bf16[144,1024]{1,0:T(8,128)(2,1)} %get-tuple-element.18), channel_id=1, source_target_pairs={{0,8},{2,10},{4,12},{6,14},{8,16},{10,18},{12,20},{14,22},{16,24},... | collective-permute-start | bytes 884744 | tf_op jit(solution)/shard_map/ppermute | solution.py:247
  471.1 1.1 copy-start.2
  472.3 14.4 %collective-permute-start.11 = (bf16[144,1152]{1,0:T(8,128)(2,1)S(1)}, bf16[144,1152]{1,0:T(8,128)(2,1)S(1)}, u32[]{:S(2)}, u32[]{:S(2)}) collective-permute-start(bf16[144,1152]{1,0:T(8,128)(2,1)S(1)} %get-tuple-element.16), channel_id=1, source_target_pairs={{0,24},{2,26},{4,28},{6,30},{8,0},{10,2},{12,4},{14,6},{16,8},{18,... | collective-permute-start | bytes 995336 | tf_op jit(solution)/shard_map/ppermute | solution.py:247
  475.7 24.6 %collective-permute-start.10 = (bf16[144,1152]{1,0:T(8,128)(2,1)S(1)}, bf16[144,1152]{1,0:T(8,128)(2,1)S(1)}, u32[]{:S(2)}, u32[]{:S(2)}) collective-permute-start(bf16[144,1152]{1,0:T(8,128)(2,1)S(1)} %get-tuple-element.17), channel_id=1, source_target_pairs={{0,16},{2,18},{4,20},{6,22},{8,24},{10,26},{12,28},{14,30},{16,0},... | collective-permute-start | bytes 995336 | tf_op jit(solution)/shard_map/ppermute | solution.py:247
  475.7 0.7 copy-start.4
  475.7 24.6 %collective-permute-start.9 = (bf16[144,1152]{1,0:T(8,128)(2,1)S(1)}, bf16[144,1152]{1,0:T(8,128)(2,1)S(1)}, u32[]{:S(2)}, u32[]{:S(2)}) collective-permute-start(bf16[144,1152]{1,0:T(8,128)(2,1)S(1)} %get-tuple-element.15), channel_id=1, source_target_pairs={{0,8},{2,10},{4,12},{6,14},{8,16},{10,18},{12,20},{14,22},{16,24},... | collective-permute-start | bytes 995336 | tf_op jit(solution)/shard_map/ppermute | solution.py:247
  511.0 15.9 %collective-permute-start.12 = (bf16[144,2304]{1,0:T(8,128)(2,1)}, bf16[144,2304]{1,0:T(8,128)(2,1)S(1)}, u32[]{:S(2)}, u32[]{:S(2)}) collective-permute-start(bf16[144,2304]{1,0:T(8,128)(2,1)} %shard_map.142), channel_id=1, source_target_pairs={{0,1},{1,0},{2,3},{3,2},{4,5},{5,4},{6,7},{7,6},{8,9},{9,8},{10,11... | collective-permute-start | bytes 1990664 | tf_op jit(solution)/shard_map/ppermute | solution.py:326
  512.4 17.3 %copy-start.6 = (bf16[2304]{0:T(1024)(128)(2,1)S(1)}, bf16[2304]{0:T(1024)(128)(2,1)}, u32[]{:S(2)}) copy-start(bf16[2304]{0:T(1024)(128)(2,1)} %param.18) | copy-start | bytes 13828
  528.2 3.6 collective-permute-start.13
Sparse Core Ops, SparseCore 0:
  10.6 190.5 all-gather.3
  218.0 98.9 all-gather.5
  318.6 145.7 all-gather.7
